TPU v7x, 512 devices: a whole 4x8x8 slice. The times are simulated.
512 devices in a mesh: mem: 16 (over y, core), tile: 32 (over z, x).
Axes of the slice: x: 4, y: 8, z: 8, core: 2. Of those that a mesh axis runs over, the one named last changes fastest.
Arguments:
- ensemble_profiles_before: bfloat16 [64, 40, 65536], P('mem', None, 'tile'), may hold values from -6 to 6
- mixing_coefficient: float32 [65536], P('tile'), may hold values from 0.05 to 0.24
- surface_driver: float32 [64, 65536], P('mem', 'tile'), may hold values from -3 to 3
- terrain_indicator: int32 [65536], P('tile'), may hold values 0 or 1
- measured_profile_position: int32 [131072], P('tile'), may hold values from 0 to 2047
- measured_field_index: int32 [131072], P('tile'), may hold values from 0 to 39
- obs_valid: int32 [131072], P('tile'), may hold values 0 or 1
- obs_value: bfloat16 [131072], P('tile'), may hold values from -6 to 6
- obs_error: bfloat16 [131072], P('tile'), may hold values from 0.5 to 4
- local_weight: float32 [16, 32, 20480], P('mem', 'tile'), may hold values from 0.001 to 0.03
Outputs:
- analysis: bfloat16 [64, 40, 65536], P('mem', None, 'tile')
All inputs are finite; a program needn't handle non-finite values. No bound on the sum of `terrain_indicator` or of `obs_valid` on one device may be relied on, other than what follows from the above.
Results may differ from a plain program's by a relative error of at most 0.0034.
Values may be sent and summed in bfloat16 or wider, within the bound.
No kernel may reach another device: no remote copies, remote signals or barrier semaphores. Data moves between devices by JAX's collectives and lax.ppermute only.
A program may use at most 64 MiB of HBM per device.

v0:
```python
import jax
import jax.numpy as jnp
from jax import lax
from jax.sharding import PartitionSpec as P

REACH = 2
NS_ITERS = 3


EXACT = lax.Precision.HIGHEST


def from_everyone(shard, axis):
    length = lax.axis_size(axis)
    return lax.all_to_all(
        jnp.broadcast_to(shard[None], (length, *shard.shape)), axis, 0, 0, tiled=True
    )


def in_order(parts, dim):
    dims = list(parts.shape[1:])
    dims[dim] *= parts.shape[0]
    return jnp.moveaxis(parts, 0, dim).reshape(dims)


def gather_directly(shard, axis, dim):
    parts = from_everyone(shard, axis)
    return in_order(parts, dim)


def from_behind(value, axis, steps):
    count = lax.axis_size(axis)
    pairs = [(source, (source + steps) % count) for source in range(count)]
    return lax.ppermute(value, axis, pairs)


def vertical_mixing_step(
    ensemble_profiles_before, mixing_coefficient, surface_driver, terrain_indicator
):
    values = ensemble_profiles_before.astype(jnp.float32)
    above_layer = jnp.concatenate([values[:, :1], values[:, :-1]], axis=1)
    below_layer = jnp.concatenate([values[:, 1:], values[:, -1:]], axis=1)
    diffused = values + mixing_coefficient[None, None, :] * (
        above_layer - 2.0 * values + below_layer
    )
    stepped = diffused - 0.05 * values * values * values
    surface = jnp.concatenate([stepped[:, :1] + surface_driver[:, None, :], stepped[:, 1:]], axis=1)
    result = jnp.where(terrain_indicator[None, None, :] > 0, surface, values)
    return result.astype(jnp.bfloat16)


def measurement_operator(background_ensemble, measured_profile_position, measured_field_index):
    profile_sequence = background_ensemble.shape[2]
    unrolled_ensemble = background_ensemble.reshape(background_ensemble.shape[0], -1)
    slot_index = measured_field_index * profile_sequence + measured_profile_position
    return jnp.take(unrolled_ensemble, slot_index, axis=1)


def prepare(window):
    ensemble_profiles = window.shape[0] - 3
    measured_quantities = window[:ensemble_profiles].astype(jnp.float32)
    average = jnp.mean(measured_quantities, axis=0)
    deviation = measured_quantities - average
    innovation = window[ensemble_profiles].astype(jnp.float32) - average
    obs_precision = window[ensemble_profiles + 2].astype(jnp.float32) / window[
        ensemble_profiles + 1
    ].astype(jnp.float32)
    return (deviation, innovation, obs_precision)


def weights_for(deviation, innovation, precision, portions):
    ensemble_profiles = deviation.shape[0]
    portion_width = deviation.shape[1] // portions
    spread = jnp.zeros((ensemble_profiles, ensemble_profiles), jnp.float32)
    for portion_index in range(portions):
        portion = deviation[:, portion_index * portion_width : (portion_index + 1) * portion_width]
        scaled = (
            portion
            * precision[None, portion_index * portion_width : (portion_index + 1) * portion_width]
        )
        spread = spread + jnp.dot(
            scaled, portion.T, precision=EXACT, preferred_element_type=jnp.float32
        )
    spread = spread / (ensemble_profiles - 1.0)
    pulled = jnp.dot(
        deviation, precision * innovation, precision=EXACT, preferred_element_type=jnp.float32
    ) / (ensemble_profiles - 1.0)
    identity = jnp.eye(ensemble_profiles, dtype=jnp.float32)
    system = identity + spread
    norm_scale = jnp.sqrt(jnp.sum(system * system))

    def newton(sweep, carry):
        current, inv_root = carry
        middle = 1.5 * identity - 0.5 * jnp.dot(inv_root, current, precision=EXACT)
        return (
            jnp.dot(current, middle, precision=EXACT),
            jnp.dot(middle, inv_root, precision=EXACT),
        )

    current, inv_root = lax.fori_loop(0, NS_ITERS, newton, (system / norm_scale, identity))
    inv_root = inv_root / jnp.sqrt(norm_scale)
    inverse = jnp.dot(inv_root, inv_root, precision=EXACT)
    mean_weight = jnp.dot(inverse, pulled, precision=EXACT)
    return inv_root + mean_weight[:, None]


def update(states, transform, land_block):
    values = states.astype(jnp.float32)
    average = jnp.mean(values, axis=0)
    deviation = values - average[None]
    moved = jnp.einsum("isc,ij->jsc", deviation, transform, precision=EXACT)
    result = jnp.where(land_block[None, None, :] > 0, average[None] + moved, values)
    return result.astype(jnp.bfloat16)


def on_device(
    ensemble_profiles_before,
    mixing_coefficient,
    surface_driver,
    terrain_indicator,
    measured_profile_position,
    measured_field_index,
    obs_valid,
    obs_value,
    obs_error,
    local_weight,
):
    background_ensemble = vertical_mixing_step(
        ensemble_profiles_before, mixing_coefficient, surface_driver, terrain_indicator
    )
    measured_quantities = measurement_operator(
        background_ensemble, measured_profile_position, measured_field_index
    )
    metadata = jnp.stack([obs_value, obs_error, obs_valid.astype(jnp.bfloat16)])
    everyone = gather_directly(measured_quantities, "mem", 0)
    own_rows = jnp.concatenate([everyone, metadata], axis=0)
    pieces = []
    for offset in range(-REACH, REACH + 1):
        if offset == 0:
            pieces.append(own_rows)
        else:
            pieces.append(from_behind(own_rows, "tile", -offset))
    window = jnp.concatenate(pieces, axis=1)
    regrouped_states = lax.all_to_all(
        background_ensemble, "mem", split_axis=2, concat_axis=0, tiled=True
    )
    deviation, innovation, obs_precision = prepare(window)
    columns_here = regrouped_states.shape[2]
    local_land = lax.dynamic_slice_in_dim(
        terrain_indicator, lax.axis_index("mem") * columns_here, columns_here
    )
    transform = weights_for(
        deviation, innovation, obs_precision * local_weight[0, 0], 2 * REACH + 1
    )
    outputs = update(regrouped_states, transform, local_land)
    return lax.all_to_all(outputs, "mem", split_axis=0, concat_axis=2, tiled=True)


def solution(mesh):
    in_specs = (
        P("mem", None, "tile"),
        P("tile"),
        P("mem", "tile"),
        P("tile"),
        P("tile"),
        P("tile"),
        P("tile"),
        P("tile"),
        P("tile"),
        P("mem", "tile", None),
    )
    out_specs = P("mem", None, "tile")
    return jax.shard_map(
        on_device, mesh=mesh, in_specs=in_specs, out_specs=out_specs, check_vma=False
    )
```

profile of v0, /device:TPU:1, one launch (start us, length us, event | category | flops | bytes accessed | tf_op | source)
XLA Modules:
  0.0 176.1 jit_solution(5342075388194978197)
XLA Ops:
  0.0 1.6 copy_convert_fusion
  1.6 0.9 fusion.58
  2.7 1.2 fusion.15
  4.0 0.3 slice.87
  4.3 0.4 copy-done.11
  4.7 0.7 fusion.19
  5.3 13.2 %copy.100 = bf16[4,40,2048]{0,2,1:T(8,128)(2,1)} copy(bf16[4,40,2048]{2,0,1:T(4,128)(2,1)S(1)} %fusion.19) | data formatting | bytes 1310720 | tf_op jit(solution)/shard_map/convert_element_type | solution.py:49
  18.6 20.7 %gather_fusion = bf16[4096,4]{1,0:T(8,128)(2,1)S(1)} fusion(bf16[4,81920]{0,1:T(8,128)(2,1)} %bitcast.63, s32[4096]{0:T(1024)S(1)} %broadcast_clamp_fusion), kind=kCustom, calls=%fused_computation | custom fusion | bytes 81920 | tf_op jit(solution)/shard_map/jit(_take)/gather | solution.py:56
  39.3 2.1 %select_bitcast_fusion = bf16[4,4096]{0,1:T(8,128)(2,1)S(1)} fusion(bf16[4096,4]{1,0:T(8,128)(2,1)S(1)} %gather_fusion, pred[4096]{0:T(1024)(128)(4,1)S(1)} %compare_and_fusion), kind=kLoop, calls=%fused_computation.45 | loop fusion | flops 16384 | bytes 69632 | tf_op jit(solution)/shard_map/jit(_take)/select_n | solution.py:56
  41.4 0.4 copy.101
  41.8 1.0 broadcast_in_dim.55
  42.8 10.2 %all-to-all-start.1 = ((bf16[16,4,4096]{2,1,0:T(4,128)(2,1)}), bf16[16,4,4096]{2,1,0:T(4,128)(2,1)S(1)}, u32[]{:S(2)}, u32[]{:S(2)}) async-start(bf16[16,4,4096]{2,1,0:T(4,128)(2,1)} %broadcast_in_dim.55), calls=%async_computation.1 | async-start | bytes 1048576 | tf_op jit(solution)/shard_map/all_to_all | solution.py:15
  53.1 1.6 copy.97
  54.6 3.9 %reshape.75 = bf16[16,2,10240]{2,1,0:T(2,128)(2,1)} reshape(bf16[2048,4,40]{2,1,0:T(4,128)(2,1)S(1)} %bitcast.65) | data formatting | bytes 1310720
  58.5 11.9 %all-to-all-done.1 = bf16[16,4,4096]{2,1,0:T(4,128)(2,1)S(1)} async-done(((bf16[16,4,4096]{2,1,0:T(4,128)(2,1)}), bf16[16,4,4096]{2,1,0:T(4,128)(2,1)S(1)}, u32[]{:S(2)}, u32[]{:S(2)}) %all-to-all-start.1) | async-done | bytes 524320 | tf_op jit(solution)/shard_map/all_to_all | solution.py:15
  70.4 3.5 %all-to-all-start = ((bf16[16,2,10240]{2,1,0:T(2,128)(2,1)}), bf16[16,2,10240]{2,1,0:T(2,128)(2,1)S(1)}, u32[]{:S(2)}, u32[]{:S(2)}) async-start(bf16[16,2,10240]{2,1,0:T(2,128)(2,1)} %reshape.75), calls=%async_computation | async-start | bytes 1310720 | tf_op jit(solution)/shard_map/all_to_all | solution.py:144
  74.2 1.0 pad_maximum_fusion
  75.1 3.0 %collective-permute-start = (bf16[67,4096]{1,0:T(8,128)(2,1)}, bf16[67,4096]{1,0:T(8,128)(2,1)}, u32[]{:S(2)}, u32[]{:S(2)}) collective-permute-start(bf16[67,4096]{1,0:T(8,128)(2,1)} %pad_maximum_fusion), channel_id=1, source_target_pairs={{0,2},{1,3},{2,4},{3,5},{4,6},{5,7},{6,8},{7,9},{8,10},{9,11},{10,... | collective-permute-start | bytes 1646600 | tf_op jit(solution)/shard_map/ppermute | solution.py:34
  78.2 2.2 %collective-permute-start.1 = (bf16[67,4096]{1,0:T(8,128)(2,1)}, bf16[67,4096]{1,0:T(8,128)(2,1)}, u32[]{:S(2)}, u32[]{:S(2)}) collective-permute-start(bf16[67,4096]{1,0:T(8,128)(2,1)} %pad_maximum_fusion), channel_id=1, source_target_pairs={{0,1},{1,2},{2,3},{3,4},{4,5},{5,6},{6,7},{7,8},{8,9},{9,10},{10,1... | collective-permute-start | bytes 1646600 | tf_op jit(solution)/shard_map/ppermute | solution.py:34
  80.4 9.8 %collective-permute-start.2 = (bf16[67,4096]{1,0:T(8,128)(2,1)}, bf16[67,4096]{1,0:T(8,128)(2,1)}, u32[]{:S(2)}, u32[]{:S(2)}) collective-permute-start(bf16[67,4096]{1,0:T(8,128)(2,1)} %pad_maximum_fusion), channel_id=1, source_target_pairs={{0,31},{1,0},{2,1},{3,2},{4,3},{5,4},{6,5},{7,6},{8,7},{9,8},{10,9... | collective-permute-start | bytes 1646600 | tf_op jit(solution)/shard_map/ppermute | solution.py:34
  90.3 4.4 %collective-permute-start.3 = (bf16[67,4096]{1,0:T(8,128)(2,1)}, bf16[67,4096]{1,0:T(8,128)(2,1)}, u32[]{:S(2)}, u32[]{:S(2)}) collective-permute-start(bf16[67,4096]{1,0:T(8,128)(2,1)} %pad_maximum_fusion), channel_id=1, source_target_pairs={{0,30},{1,31},{2,0},{3,1},{4,2},{5,3},{6,4},{7,5},{8,6},{9,7},{10,... | collective-permute-start | bytes 1646600 | tf_op jit(solution)/shard_map/ppermute | solution.py:34
  94.7 3.3 %reshape.76 = bf16[2048,4,40]{2,1,0:T(4,128)(2,1)S(1)} reshape(bf16[16,2,10240]{2,1,0:T(2,128)(2,1)S(1)} %all-to-all-done) | data formatting | bytes 1310720
  98.1 7.6 %convert_reduce_fusion.1 = f32[40,2048]{0,1:T(8,128)S(1)} fusion(bf16[2048,4,40]{2,1,0:T(4,128)(2,1)S(1)} %reshape.76), kind=kLoop, calls=%fused_computation.46 | loop fusion | flops 573440 | bytes 983040 | tf_op jit(solution)/shard_map/reduce_sum | solution.py:109
  105.9 1.3 copy.103
  107.2 1.2 constant_dynamic-update-slice_fusion.4
  108.4 6.3 %collective-permute-done.1 = bf16[67,4096]{1,0:T(8,128)(2,1)} collective-permute-done((bf16[67,4096]{1,0:T(8,128)(2,1)}, bf16[67,4096]{1,0:T(8,128)(2,1)}, u32[]{:S(2)}, u32[]{:S(2)}) %collective-permute-start.1) | collective-permute-done | bytes 548896 | tf_op jit(solution)/shard_map/ppermute | solution.py:34
  114.7 1.1 constant_dynamic-update-slice_fusion.3
  115.9 14.4 %collective-permute-done.2 = bf16[67,4096]{1,0:T(8,128)(2,1)} collective-permute-done((bf16[67,4096]{1,0:T(8,128)(2,1)}, bf16[67,4096]{1,0:T(8,128)(2,1)}, u32[]{:S(2)}, u32[]{:S(2)}) %collective-permute-start.2) | collective-permute-done | bytes 548896 | tf_op jit(solution)/shard_map/ppermute | solution.py:34
  130.3 1.1 constant_dynamic-update-slice_fusion.1
  131.4 1.1 constant_dynamic-update-slice_fusion
  132.8 0.5 convert_reduce_fusion
  133.2 0.4 copy-done.3
  133.7 0.4 convert_subtract_fusion
  134.1 4.2 %fusion.40 = f32[64,1]{0,1:T(1,128)S(1)} fusion(f32[20480,1]{0,1:T(1,128)S(1)} %bitcast.72, f32[20480]{0:T(1024)S(1)} %get-tuple-element.74, bf16[67,20480]{1,0:T(8,128)(2,1)S(1)} %constant_dynamic-update-slice_fusion), kind=kOutput, calls=%fused_computation.39 | convolution fusion | flops 18350144 | bytes 2785536 | tf_op jit(solution)/shard_map/dot_general | solution.py:85
  138.3 1.0 fusion.9
  139.4 1.0 fusion.7
  140.4 1.0 fusion.5
  141.4 1.0 fusion.3
  142.4 1.6 multiply_reduce_fusion
  144.9 1.9 %while.13 = (s32[]{:T(128)}, f32[64,64]{0,1:T(8,128)S(1)}, f32[64,64]{1,0:T(8,128)S(1)}, s32[]{:T(128)}) while((s32[]{:T(128)}, f32[64,64]{0,1:T(8,128)S(1)}, f32[64,64]{1,0:T(8,128)S(1)}, s32[]{:T(128)}) %tuple.37), condition=%wide.region_5.6_spmd.clone, body=%wide.region_4.5_spmd.clone.sunk | while | flops 9453570 | bytes 213045 | solution.py:100
  144.9 0.2 fusion.85
  145.3 0.2 convolution_bitcast_fusion.4
  145.9 0.2 convolution_bitcast_fusion.4
  146.6 0.2 convolution_bitcast_fusion.4
  147.1 1.4 fusion.14
  148.5 0.4 copy.105
  149.0 26.2 %all_to_all.32 = bf16[64,40,128]{2,1,0:T(8,128)(2,1)S(1)} all-to-all(bf16[64,40,128]{2,1,0:T(8,128)(2,1)S(1)} %copy.105), channel_id=1, replica_groups=mesh['mem'=16,'tile'=32] {'mem'}, dimensions={0} | all-to-all | bytes 1310720 | tf_op jit(solution)/shard_map/all_to_all | solution.py:156
  175.1 1.0 copy.117
  (60 shorter events, 2.2 us)
Async XLA Ops:
  1.6 0.9 copy-start.4
  1.6 0.9 copy-start.5
  1.6 1.1 copy-start
  1.6 1.1 copy-start.8
  2.7 1.5 copy-start.6
  4.0 0.7 copy-start.11
  42.8 27.6 %all-to-all-start.1 = ((bf16[16,4,4096]{2,1,0:T(4,128)(2,1)}), bf16[16,4,4096]{2,1,0:T(4,128)(2,1)S(1)}, u32[]{:S(2)}, u32[]{:S(2)}) async-start(bf16[16,4,4096]{2,1,0:T(4,128)(2,1)} %broadcast_in_dim.55), calls=%async_computation.1 | async-start | bytes 1048576 | tf_op jit(solution)/shard_map/all_to_all | solution.py:15
  58.5 15.4 %copy-start.7 = (s32[4096]{0:T(1024)S(1)}, s32[4096]{0:T(1024)}, u32[]{:S(2)}) copy-start(s32[4096]{0:T(1024)} %param.18) | copy-start | bytes 49156
  58.5 15.4 %copy-start.9 = (bf16[4096]{0:T(1024)(128)(2,1)S(1)}, bf16[4096]{0:T(1024)(128)(2,1)}, u32[]{:S(2)}) copy-start(bf16[4096]{0:T(1024)(128)(2,1)} %param.20) | copy-start | bytes 24580
  58.5 15.5 %copy-start.10 = (bf16[4096]{0:T(1024)(128)(2,1)S(1)}, bf16[4096]{0:T(1024)(128)(2,1)}, u32[]{:S(2)}) copy-start(bf16[4096]{0:T(1024)(128)(2,1)} %param.19) | copy-start | bytes 24580
  70.4 24.3 %all-to-all-start = ((bf16[16,2,10240]{2,1,0:T(2,128)(2,1)}), bf16[16,2,10240]{2,1,0:T(2,128)(2,1)S(1)}, u32[]{:S(2)}, u32[]{:S(2)}) async-start(bf16[16,2,10240]{2,1,0:T(2,128)(2,1)} %reshape.75), calls=%async_computation | async-start | bytes 1310720 | tf_op jit(solution)/shard_map/all_to_all | solution.py:144
  74.2 20.6 %copy-start.1 = (bf16[64,4096]{1,0:T(8,128)(2,1)}, bf16[64,4096]{1,0:T(8,128)(2,1)S(1)}, u32[]{:S(2)}) copy-start(bf16[64,4096]{1,0:T(8,128)(2,1)S(1)} %reshape.57) | copy-start | bytes 1572868
  75.1 32.1 %collective-permute-start = (bf16[67,4096]{1,0:T(8,128)(2,1)}, bf16[67,4096]{1,0:T(8,128)(2,1)}, u32[]{:S(2)}, u32[]{:S(2)}) collective-permute-start(bf16[67,4096]{1,0:T(8,128)(2,1)} %pad_maximum_fusion), channel_id=1, source_target_pairs={{0,2},{1,3},{2,4},{3,5},{4,6},{5,7},{6,8},{7,9},{8,10},{9,11},{10,... | collective-permute-start | bytes 1646600 | tf_op jit(solution)/shard_map/ppermute | solution.py:34
  78.2 36.5 %collective-permute-start.1 = (bf16[67,4096]{1,0:T(8,128)(2,1)}, bf16[67,4096]{1,0:T(8,128)(2,1)}, u32[]{:S(2)}, u32[]{:S(2)}) collective-permute-start(bf16[67,4096]{1,0:T(8,128)(2,1)} %pad_maximum_fusion), channel_id=1, source_target_pairs={{0,1},{1,2},{2,3},{3,4},{4,5},{5,6},{6,7},{7,8},{8,9},{9,10},{10,1... | collective-permute-start | bytes 1646600 | tf_op jit(solution)/shard_map/ppermute | solution.py:34
  80.4 49.9 %collective-permute-start.2 = (bf16[67,4096]{1,0:T(8,128)(2,1)}, bf16[67,4096]{1,0:T(8,128)(2,1)}, u32[]{:S(2)}, u32[]{:S(2)}) collective-permute-start(bf16[67,4096]{1,0:T(8,128)(2,1)} %pad_maximum_fusion), channel_id=1, source_target_pairs={{0,31},{1,0},{2,1},{3,2},{4,3},{5,4},{6,5},{7,6},{8,7},{9,8},{10,9... | collective-permute-start | bytes 1646600 | tf_op jit(solution)/shard_map/ppermute | solution.py:34
  90.3 41.1 %collective-permute-start.3 = (bf16[67,4096]{1,0:T(8,128)(2,1)}, bf16[67,4096]{1,0:T(8,128)(2,1)}, u32[]{:S(2)}, u32[]{:S(2)}) collective-permute-start(bf16[67,4096]{1,0:T(8,128)(2,1)} %pad_maximum_fusion), channel_id=1, source_target_pairs={{0,30},{1,31},{2,0},{3,1},{4,2},{5,3},{6,4},{7,5},{8,6},{9,7},{10,... | collective-permute-start | bytes 1646600 | tf_op jit(solution)/shard_map/ppermute | solution.py:34
  107.2 8.6 %copy-start.2 = (bf16[64,4096]{1,0:T(8,128)(2,1)S(1)}, bf16[64,4096]{1,0:T(8,128)(2,1)}, u32[]{:S(2)}) copy-start(bf16[64,4096]{1,0:T(8,128)(2,1)} %copy-done.1) | copy-start | bytes 1572868
  132.7 0.9 copy-start.3
where the time goes:
time: 177 us; the launch traced here: 176 us
  local copies, waits for them, and re-layouts  53.7 us (30%)
  starting transfers between devices  33.2 us (19%)
  waiting for transfers between devices  32.6 us (18%)
  blocking collectives  26.2 us (15%)
  other arithmetic  15.7 us (9%)
  matrix products  13.4 us (8%)
    all_to_all x1, blocking collectives, on_device(): lax.all_to_all(outputs, 'mem', split_axis=0, concat_axis=2, tiled=True)  26.2 us
    ppermute x4, waiting for transfers between devices, from_behind(): return lax.ppermute(value, axis, pairs)  20.7 us
    gather x1, local copies, waits for them, and re-layouts, measurement_operator(): return jnp.take(unrolled_ensemble, slot_index, axis=1)  20.7 us
    ppermute x4, starting transfers between devices, from_behind(): return lax.ppermute(value, axis, pairs)  19.5 us
    convert_element_type x2, local copies, waits for them, and re-layouts, vertical_mixing_step(): return result.astype(jnp.bfloat16)  14.8 us
    all_to_all x1, waiting for transfers between devices, from_everyone(): lax.all_to_all(jnp.broadcast_to(shard[None], (length, *shard.shape)), axi...  11.9 us
    unnamed x30, local copies, waits for them, and re-layouts  11.6 us
    all_to_all x1, starting transfers between devices, from_everyone(): lax.all_to_all(jnp.broadcast_to(shard[None], (length, *shard.shape)), axi...  10.2 us
  transfers between devices with their start and end apart: 6, of which 3 were waited for; matrix products, arithmetic and copies ran while one was open for 13% of the time, Pallas kernels for 0%

commit v1 on v0

v1 whole, which is shorter than its diff:
```python
import jax
import jax.numpy as jnp
from jax import lax
from jax.experimental import pallas as pl
from jax.experimental.pallas import tpu as pltpu
from jax.sharding import PartitionSpec as P

REACH = 2
NS_ITERS = 3

F32 = jnp.float32
BF16 = jnp.bfloat16
EXACT = lax.Precision.HIGHEST
VMEM_LIMIT = 40 * 1024 * 1024

MEM = 16
OWN = 4
LAYERS = 40
LANE = 128
ROWS = OWN * LAYERS
MEMBERS = MEM * OWN
PARTS = 4
PART_COLS = 2048 // PARTS
HALF = 16
GROUP = 4
PACK = 40


def call(kernel, out_shape, scratch, flops, nbytes, *args):
    vmem = pl.BlockSpec(memory_space=pltpu.VMEM)
    return pl.pallas_call(
        kernel,
        out_shape=out_shape,
        in_specs=[vmem] * len(args),
        out_specs=jax.tree.map(lambda _: vmem, out_shape),
        scratch_shapes=scratch,
        compiler_params=pltpu.CompilerParams(vmem_limit_bytes=VMEM_LIMIT),
        cost_estimate=pl.CostEstimate(flops=flops, bytes_accessed=nbytes, transcendentals=0),
    )(*args)


def forecast_kernel(
    x_ref, mix_ref, drive_ref, land_ref, pos_ref, field_ref, states_ref, seen_ref, table, seen
):
    layer = lax.broadcasted_iota(jnp.int32, (LAYERS, LANE), 0)
    for block in range(MEM):
        lanes = slice(block * LANE, (block + 1) * LANE)
        mix = mix_ref[block : block + 1, :]
        land = jnp.broadcast_to(land_ref[block : block + 1, :], (LAYERS, LANE)) > 0
        members = []
        for k in range(OWN):
            x = x_ref[k, :, lanes].astype(F32)
            above = jnp.where(layer == 0, x, pltpu.roll(x, 1, 0))
            below = jnp.where(layer == LAYERS - 1, x, pltpu.roll(x, LAYERS - 1, 0))
            stepped = x + mix * (above - 2.0 * x + below) - 0.05 * x * x * x
            stepped = jnp.where(layer == 0, stepped + drive_ref[k : k + 1, lanes], stepped)
            members.append(jnp.where(land, stepped, x))
        result = jnp.concatenate(members, axis=0).astype(BF16)
        states_ref[block] = result
        part, place = divmod(block, MEM // PARTS)
        table[part * ROWS : (part + 1) * ROWS, place * LANE : (place + 1) * LANE] = result

    column = lax.broadcasted_iota(jnp.int32, (PART_COLS, LANE), 0)
    for pair in range(HALF):
        hot, codes = [], []
        for row in (2 * pair, 2 * pair + 1):
            pos = pos_ref[row : row + 1, :]
            hot.append(jnp.where(column == (pos & (PART_COLS - 1)), 1.0, 0.0).astype(BF16))
            codes.append((pos // PART_COLS) * LAYERS + field_ref[row : row + 1, :])
        found = jnp.dot(table[...], jnp.concatenate(hot, axis=1), preferred_element_type=F32)
        for i in range(2):
            half, place = divmod(2 * pair + i, HALF)
            hits = [layer == codes[i] - part * LAYERS for part in range(PARTS)]
            for k in range(OWN):
                total = jnp.zeros((LAYERS, LANE), F32)
                for part in range(PARTS):
                    first = part * ROWS + k * LAYERS
                    total = jnp.where(
                        hits[part],
                        found[first : first + LAYERS, i * LANE : (i + 1) * LANE],
                        total,
                    )
                at = half * OWN * HALF + k * HALF + place
                seen[at : at + 1, :] = jnp.sum(total, axis=0, keepdims=True)
    for half in range(2):
        values = seen[half * OWN * HALF : (half + 1) * OWN * HALF, :].astype(BF16)
        for chip in range(MEM // 2):
            seen_ref[2 * chip + half] = values


def group_places():
    tile = lax.axis_index("tile")
    return tile % GROUP, (tile + GROUP // 2) % GROUP


def sums_kernel(
    seen_ref, w1_ref, w2_ref, value_ref, error_ref, valid_ref, p1_ref, p2_ref, wide, dev_s, inn_s, scaled
):
    core = lax.axis_index("mem") % 2
    _, place2 = group_places()
    across = jnp.where(place2 < 2, 4, 0)
    wide[...] = seen_ref[...].reshape(MEM * OWN * HALF, LANE).astype(F32)
    start = pl.multiple_of(core * HALF, HALF)
    obs_value = value_ref[pl.ds(start, HALF), :].astype(F32)
    base = valid_ref[pl.ds(start, HALF), :].astype(F32) / error_ref[pl.ds(start, HALF), :].astype(F32)
    first_row = lax.broadcasted_iota(jnp.int32, (16, LANE), 0) == 0
    for row in range(HALF):
        lanes = slice(row * LANE, (row + 1) * LANE)
        values = wide[pl.ds(row, MEMBERS, stride=HALF), :]
        mean = jnp.sum(values, axis=0, keepdims=True) * (1.0 / MEMBERS)
        deviation = values - mean
        rounded = deviation.astype(BF16)
        dev_s[0:MEMBERS, lanes] = rounded
        dev_s[MEMBERS : 2 * MEMBERS, lanes] = rounded
        innovation = obs_value[row : row + 1, :] - mean
        inn_s[:, lanes] = jnp.where(first_row, innovation, 0.0).astype(BF16)
        for j in range(12):
            weight = w1_ref[j, row : row + 1, :] if j < 8 else w2_ref[across + (j - 8), row : row + 1, :]
            rinv = base[row : row + 1, :] * weight
            scaled[j * MEMBERS : (j + 1) * MEMBERS, lanes] = (deviation * rinv).astype(BF16)
    last = (((1,), (1,)), ((), ()))
    spread = lax.dot_general(scaled[...], dev_s[...], last, preferred_element_type=F32)
    pulled = lax.dot_general(inn_s[...], scaled[...], last, preferred_element_type=F32)
    left = lax.broadcasted_iota(jnp.int32, (32, LANE), 1) < MEMBERS
    p2_ref[...] = jnp.zeros_like(p2_ref)
    for j in range(12):
        top = spread[j * MEMBERS : j * MEMBERS + 32, :]
        bottom = spread[j * MEMBERS + 32 : (j + 1) * MEMBERS, :]
        packed = jnp.where(left, top, bottom)
        pull = pulled[0:8, (j // 2) * LANE : (j // 2 + 1) * LANE]
        if j < 8:
            p1_ref[j, 0:32, :] = packed
            p1_ref[j, 32:40, :] = pull
        else:
            p2_ref[across + (j - 8), 0:32, :] = packed
            p2_ref[across + (j - 8), 32:40, :] = pull


def regroup_kernel(states_ref, out_ref, wide):
    wide[...] = states_ref[...].reshape(MEM * ROWS, LANE).astype(F32)
    for layer in range(LAYERS):
        out_ref[:, layer * LANE : (layer + 1) * LANE] = wide[
            pl.ds(layer, MEMBERS, stride=LAYERS), :
        ].astype(BF16)


def exact_dot(a, b):
    return jnp.dot(a, b, precision=EXACT, preferred_element_type=F32)


def update_kernel(p1_ref, p2_ref, states_ref, land_ref, out_ref, wide):
    block = lax.axis_index("mem")
    core = block % 2
    place1, place2 = group_places()
    total = jnp.zeros((PACK, LANE), F32)
    for j in range(2 * GROUP):
        q = j // 2
        near = jnp.abs(q - place1) <= REACH
        total = total + jnp.where(near, p1_ref[j], 0.0)
    for j in range(2 * GROUP):
        q = j // 2
        other = (place2 >= 2) if q < 2 else (place2 < 2)
        near = jnp.logical_and(other, jnp.abs(q - place2) <= REACH)
        total = total + jnp.where(near, p2_ref[j], 0.0)
    total = total * (1.0 / (MEMBERS - 1.0))
    upper = total[0:32, :]
    spread = jnp.concatenate([upper, pltpu.roll(upper, MEMBERS, 1)], axis=0)[:, :MEMBERS]
    pull = total[32:40, :]
    pull = jnp.where(core == 0, pull, pltpu.roll(pull, MEMBERS, 1))[:, :MEMBERS]

    rows = lax.broadcasted_iota(jnp.int32, (MEMBERS, MEMBERS), 0)
    cols = lax.broadcasted_iota(jnp.int32, (MEMBERS, MEMBERS), 1)
    identity = jnp.where(rows == cols, 1.0, 0.0)
    system = identity + spread
    square = jnp.sum(jnp.sum(system * system, axis=1, keepdims=True), axis=0, keepdims=True)
    inv_scale = lax.rsqrt(square)
    current = system * inv_scale
    root = 1.5 * identity - 0.5 * current
    current = exact_dot(current, root)
    for sweep in range(1, NS_ITERS):
        middle = 1.5 * identity - 0.5 * exact_dot(root, current)
        if sweep < NS_ITERS - 1:
            current = exact_dot(current, middle)
        root = exact_dot(middle, root)
    inv_root = root * jnp.sqrt(inv_scale)
    mean_weight = exact_dot(exact_dot(pull, inv_root), inv_root)[0:1, :]
    turned = inv_root + mean_weight
    turned = turned + (1.0 - jnp.sum(turned, axis=1, keepdims=True)) * (1.0 / MEMBERS)
    high = turned.astype(BF16)
    low = (turned - high.astype(F32)).astype(BF16)
    both = jnp.concatenate([high, low], axis=0)
    land = jnp.broadcast_to(land_ref[pl.ds(block, 1), :], (MEMBERS, LANE)) > 0
    moved = jnp.dot(both, states_ref[...], preferred_element_type=F32)
    for layer in range(LAYERS):
        lanes = slice(layer * LANE, (layer + 1) * LANE)
        result = jnp.where(
            land,
            moved[:MEMBERS, lanes] + moved[MEMBERS:, lanes],
            states_ref[:, lanes].astype(F32),
        )
        wide[pl.ds(layer, MEMBERS, stride=LAYERS), :] = result
    out_ref[...] = wide[...].astype(BF16).reshape(MEM, ROWS, LANE)


def shape(*dims, dtype=BF16):
    return jax.ShapeDtypeStruct(dims, dtype)


def exchange_groups(tiles, first):
    return [
        [
            (2 * chip + core) * tiles + (start + q) % tiles
            for q in range(GROUP)
            for core in range(2)
        ]
        for chip in range(MEM // 2)
        for start in range(first, tiles + first, GROUP)
    ]


def group_exchange(parts, groups):
    return lax.all_to_all(parts, ("mem", "tile"), 0, 0, axis_index_groups=groups, tiled=True)


def on_device(
    ensemble_profiles_before,
    mixing_coefficient,
    surface_driver,
    terrain_indicator,
    measured_profile_position,
    measured_field_index,
    obs_valid,
    obs_value,
    obs_error,
    local_weight,
):
    tiles = lax.axis_size("tile")
    groups1, groups2 = exchange_groups(tiles, 0), exchange_groups(tiles, GROUP // 2)
    place1, place2 = group_places()
    land = terrain_indicator.reshape(MEM, LANE)

    slabs = local_weight.reshape(2 * REACH + 1, 2 * HALF, LANE)
    slabs = jnp.pad(slabs, ((1, 1), (0, 0), (0, 0)))
    for_group1 = lax.dynamic_slice_in_dim(slabs, 3 - place1, GROUP).reshape(2 * GROUP, HALF, LANE)
    for_group2 = lax.dynamic_slice_in_dim(slabs, 3 - place2, GROUP).reshape(2 * GROUP, HALF, LANE)

    states, seen = call(
        forecast_kernel,
        (shape(MEM, ROWS, LANE), shape(MEM, OWN * HALF, LANE)),
        [pltpu.VMEM((PARTS * ROWS, PART_COLS), BF16), pltpu.VMEM((2 * OWN * HALF, LANE), F32)],
        2 * 4096 * ROWS * 2048,
        2000000,
        ensemble_profiles_before,
        mixing_coefficient.reshape(MEM, LANE),
        surface_driver,
        land,
        measured_profile_position.reshape(2 * HALF, LANE),
        measured_field_index.reshape(2 * HALF, LANE),
    )
    seen = lax.all_to_all(seen, "mem", 0, 0, tiled=True)
    weights1 = group_exchange(for_group1, groups1)
    weights2 = group_exchange(for_group2, groups2)
    states = lax.all_to_all(states, "mem", 0, 0, tiled=True)

    sums1, sums2 = call(
        sums_kernel,
        (shape(2 * GROUP, PACK, LANE, dtype=F32), shape(2 * GROUP, PACK, LANE, dtype=F32)),
        [
            pltpu.VMEM((MEM * OWN * HALF, LANE), F32),
            pltpu.VMEM((2 * MEMBERS, HALF * LANE), BF16),
            pltpu.VMEM((16, HALF * LANE), BF16),
            pltpu.VMEM((12 * MEMBERS, HALF * LANE), BF16),
        ],
        2 * 768 * 128 * 2048,
        1000000,
        seen,
        weights1,
        weights2,
        obs_value.reshape(2 * HALF, LANE),
        obs_error.reshape(2 * HALF, LANE),
        obs_valid.reshape(2 * HALF, LANE),
    )
    sums1 = group_exchange(sums1, groups1)
    sums2 = group_exchange(sums2, groups2)
    states = call(
        regroup_kernel,
        shape(MEMBERS, LAYERS * LANE),
        [pltpu.VMEM((MEM * ROWS, LANE), F32)],
        MEM * ROWS * LANE,
        1300000,
        states,
    )
    analysed = call(
        update_kernel,
        shape(MEM, ROWS, LANE),
        [pltpu.VMEM((MEM * ROWS, LANE), F32)],
        2 * 128 * 64 * 5120,
        1300000,
        sums1,
        sums2,
        states,
        land,
    )
    analysed = lax.all_to_all(analysed, "mem", 0, 0, tiled=True)
    return (
        analysed.reshape(MEM, OWN, LAYERS, LANE)
        .transpose(1, 2, 0, 3)
        .reshape(OWN, LAYERS, MEM * LANE)
    )


def solution(mesh):
    in_specs = (
        P("mem", None, "tile"),
        P("tile"),
        P("mem", "tile"),
        P("tile"),
        P("tile"),
        P("tile"),
        P("tile"),
        P("tile"),
        P("tile"),
        P("mem", "tile", None),
    )
    out_specs = P("mem", None, "tile")
    return jax.shard_map(
        on_device, mesh=mesh, in_specs=in_specs, out_specs=out_specs, check_vma=False
    )
```

time: 177 us -> 121 us (0.68)
  blocking collectives: 26.2 us -> 88.5 us
  local copies, waits for them, and re-layouts: 53.7 us -> 3.65 us
  waiting for transfers between devices: 32.6 us -> 2.76 us
  starting transfers between devices: 33.2 us -> 16.4 us
  other arithmetic: 15.7 us -> 0 us
  matrix products: 13.4 us -> 0 us
  Pallas kernels: 0 us -> 9.02 us
    all_to_all x1 -> x5, blocking collectives: 26.2 us -> 88.5 us  [the longest x1 24.2 us: on_device(): states = lax.all_to_all(states, 'mem', 0, 0, tiled=True)]
    ppermute x4 -> x0, waiting for transfers between devices: 20.7 us -> none  [from_behind(): return lax.ppermute(value, axis, pairs)]
    gather x1 -> x0, local copies, waits for them, and re-layouts: 20.7 us -> none  [measurement_operator(): return jnp.take(unrolled_ensemble, slot_index, axis=1)]
    ppermute x4 -> x0, starting transfers between devices: 19.5 us -> none  [from_behind(): return lax.ppermute(value, axis, pairs)]
    convert_element_type x4 -> x0, local copies, waits for them, and re-layouts: 16.6 us -> none  [the longest x2 14.8 us: vertical_mixing_step(): return result.astype(jnp.bfloat16)]
    dot_general x18 -> x0, matrix products: 13.4 us -> none  [the longest x5 5.67 us: weights_for(): jnp.dot(scaled, portion.T, precision=EXACT, preferred_element_type=jnp.fl...]
    unnamed x30 -> x18, local copies, waits for them, and re-layouts: 11.6 us -> 1.12 us
    all_to_all x2, waiting for transfers between devices: 11.9 us -> 2.76 us  [group_exchange(): lax.all_to_all(parts, ('mem', 'tile'), 0, 0, axis_index_groups=groups, ti...]
  transfers between devices with their start and end apart: 6 -> 2, of which waited for: 3 -> 1; matrix products, arithmetic and copies ran while one was open for 13% -> 0% of each run, Pallas kernels for 0% -> 4%
where the time goes in v1:
time: 121 us; the launch traced here: 120 us
  blocking collectives  88.5 us (73%)
  starting transfers between devices  16.4 us (14%)
  Pallas kernels  9.02 us (7%)
  local copies, waits for them, and re-layouts  3.65 us (3%)
  waiting for transfers between devices  2.76 us (2%)
    all_to_all x1, blocking collectives, on_device(): states = lax.all_to_all(states, 'mem', 0, 0, tiled=True)  24.2 us
    all_to_all x1, blocking collectives, on_device(): analysed = lax.all_to_all(analysed, 'mem', 0, 0, tiled=True)  23.5 us
    all_to_all x2, blocking collectives, group_exchange(): lax.all_to_all(parts, ('mem', 'tile'), 0, 0, axis_index_groups=groups, ti...  21.6 us
    all_to_all x1, blocking collectives, on_device(): seen = lax.all_to_all(seen, 'mem', 0, 0, tiled=True)  19.1 us
    all_to_all x2, starting transfers between devices, group_exchange(): lax.all_to_all(parts, ('mem', 'tile'), 0, 0, axis_index_groups=groups, ti...  16.4 us
    pallas_call x4, Pallas kernels, call(): pl.pallas_call(kernel, out_shape=out_shape, in_specs=[vmem] * len(args),...  9.02 us
    all_to_all x2, waiting for transfers between devices, group_exchange(): lax.all_to_all(parts, ('mem', 'tile'), 0, 0, axis_index_groups=groups, ti...  2.76 us
  transfers between devices with their start and end apart: 2, of which 1 were waited for; matrix products, arithmetic and copies ran while one was open for 0% of the time, Pallas kernels for 4%

profile of v1, /device:TPU:1, one launch (start us, length us, event | category | flops | bytes accessed | tf_op | source)
XLA Modules:
  0.0 120.4 jit_solution(389449236247259319)
XLA Ops:
  0.0 1.5 %pad_dynamic-slice_fusion = (f32[4,32,128]{2,1,0:T(8,128)}, f32[4,32,128]{2,1,0:T(8,128)S(1)}) fusion(s32[]{:T(128)S(6)} %select_n.20, f32[5,32,128]{2,1,0:T(8,128)} %bitcast.27, s32[]{:T(128)S(6)} %select_n.18), kind=kLoop, calls=%fused_computation.1 | loop fusion | bytes 213000 | tf_op jit(solution)/shard_map/dynamic_slice | solution.py:245
  1.5 14.1 %all_to_all.35.w1_ref = f32[8,16,128]{2,1,0:T(8,128)S(1)} all-to-all(f32[8,16,128]{2,1,0:T(8,128)S(1)} %bitcast.26), channel_id=1, replica_groups={{0,32,1,33,2,34,3,35},{4,36,5,37,6,38,7,39},{8,40,9,41,10,42,11,43},{12..., dimensions={0} | all-to-all | bytes 131072 | tf_op jit(solution)/shard_map/all_to_all | solution.py:222
  15.6 0.0 copy-start
  15.6 0.0 copy-start.2
  15.6 0.0 copy-start.3
  15.6 0.0 copy-start.4
  15.6 0.0 copy-start.6
  15.6 9.7 %all-to-all-start.2 = ((f32[8,16,128]{2,1,0:T(8,128)}), f32[8,16,128]{2,1,0:T(8,128)S(1)}, u32[]{:S(2)}, u32[]{:S(2)}) async-start(f32[8,16,128]{2,1,0:T(8,128)} %bitcast.6), calls=%async_computation.2 | async-start | bytes 131072 | tf_op jit(solution)/shard_map/all_to_all | solution.py:222
  25.3 0.0 copy-done
  25.3 0.0 copy-done.2
  25.3 0.0 copy-done.3
  25.3 0.0 copy-done.4
  25.4 0.0 copy-done.6
  25.4 0.0 copy-start.1
  25.4 1.1 copy-done.1
  26.5 4.0 %shard_map.100 = (bf16[16,160,128]{2,1,0:T(8,128)(2,1)S(1)}, bf16[16,64,128]{2,1,0:T(8,128)(2,1)S(1)}) custom-call(bf16[4,40,2048]{2,1,0:T(8,128)(2,1)S(1)} %copy-done.1, f32[16,128]{1,0:T(8,128)S(1)} %bitcast.22, f32[4,2048]{1,0:T(4,128)S(1)} %copy-done.2, s32[16,128]{1,0:T(8,128)S(1)} %bitcast.17, s32[32,128]{1,0:T(8,128)S(1)} %bitcast.19, ...), custom_call_target="tpu_custom_call" | custom-call | flops 2684354560 | bytes 2000000 | tf_op jit(solution)/shard_map/pallas_call | solution.py:31
  30.5 0.0 all-to-all-done.2.w2_ref
  30.5 0.0 copy-start.5
  30.5 0.0 copy-start.7
  30.5 0.0 copy-start.8
  30.5 19.1 %all_to_all.36.seen_ref = bf16[16,64,128]{2,1,0:T(8,128)(2,1)S(1)} all-to-all(bf16[16,64,128]{2,1,0:T(8,128)(2,1)S(1)} %get-tuple-element.9), channel_id=1, replica_groups=mesh['mem'=16,'tile'=32] {'mem'}, dimensions={0} | all-to-all | bytes 524288 | tf_op jit(solution)/shard_map/all_to_all | solution.py:260
  49.6 0.0 copy-done.5
  49.6 0.0 copy-done.7
  49.6 0.0 copy-done.8
  49.6 2.7 %shard_map.101 = (f32[8,40,128]{2,1,0:T(8,128)S(1)}, f32[8,40,128]{2,1,0:T(8,128)}) custom-call(bf16[16,64,128]{2,1,0:T(8,128)(2,1)S(1)} %all_to_all.36.seen_ref, f32[8,16,128]{2,1,0:T(8,128)S(1)} %all_to_all.35.w1_ref, f32[8,16,128]{2,1,0:T(8,128)S(1)} %all-to-all-done.2.w2_ref, bf16[32,128]{1,0:T(8,128)(2,1)S(1)} %bitcast.23, ...), custom_call_target="tpu_custom_call" | custom-call | flops 402653184 | bytes 1000000 | tf_op jit(solution)/shard_map/pallas_call | solution.py:31
  52.3 7.5 %all_to_all.37.p1_ref = f32[8,40,128]{2,1,0:T(8,128)S(1)} all-to-all(f32[8,40,128]{2,1,0:T(8,128)S(1)} %get-tuple-element.10), channel_id=1, replica_groups={{0,32,1,33,2,34,3,35},{4,36,5,37,6,38,7,39},{8,40,9,41,10,42,11,43},{12..., dimensions={0} | all-to-all | bytes 327680 | tf_op jit(solution)/shard_map/all_to_all | solution.py:222
  59.9 24.2 %all_to_all.38.states_ref = bf16[16,160,128]{2,1,0:T(8,128)(2,1)S(1)} all-to-all(bf16[16,160,128]{2,1,0:T(8,128)(2,1)S(1)} %get-tuple-element.12), channel_id=1, replica_groups=mesh['mem'=16,'tile'=32] {'mem'}, dimensions={0} | all-to-all | bytes 1310720 | tf_op jit(solution)/shard_map/all_to_all | solution.py:263
  84.1 6.7 %all-to-all-start.4 = ((f32[8,40,128]{2,1,0:T(8,128)}), f32[8,40,128]{2,1,0:T(8,128)S(1)}, u32[]{:S(2)}, u32[]{:S(2)}) async-start(f32[8,40,128]{2,1,0:T(8,128)} %get-tuple-element.11), calls=%async_computation.4 | async-start | bytes 327680 | tf_op jit(solution)/shard_map/all_to_all | solution.py:222
  90.8 0.3 shard_map.102.states_ref
  91.1 2.8 %all-to-all-done.4.p2_ref = f32[8,40,128]{2,1,0:T(8,128)S(1)} async-done(((f32[8,40,128]{2,1,0:T(8,128)}), f32[8,40,128]{2,1,0:T(8,128)S(1)}, u32[]{:S(2)}, u32[]{:S(2)}) %all-to-all-start.4) | async-done | bytes 163872 | tf_op jit(solution)/shard_map/all_to_all | solution.py:222
  93.9 2.0 %shard_map.103 = bf16[16,160,128]{2,1,0:T(8,128)(2,1)S(1)} custom-call(f32[8,40,128]{2,1,0:T(8,128)S(1)} %all_to_all.37.p1_ref, f32[8,40,128]{2,1,0:T(8,128)S(1)} %all-to-all-done.4.p2_ref, bf16[64,5120]{1,0:T(8,128)(2,1)S(1)} %shard_map.102.states_ref, s32[16,128]{1,0:T(8,128)S(1)} %bitcast.18), custom_call_target="tpu_custom_call" | custom-call | flops 83886080 | bytes 1300000 | tf_op jit(solution)/shard_map/pallas_call | solution.py:31
  95.8 23.5 %all_to_all.39 = bf16[16,160,128]{2,1,0:T(8,128)(2,1)S(1)} all-to-all(bf16[16,160,128]{2,1,0:T(8,128)(2,1)S(1)} %shard_map.103), channel_id=1, replica_groups=mesh['mem'=16,'tile'=32] {'mem'}, dimensions={0} | all-to-all | bytes 1310720 | tf_op jit(solution)/shard_map/all_to_all | solution.py:304
  119.3 1.0 copy.14
Async XLA Ops:
  15.6 9.7 %copy-start = (s32[2048]{0:T(1024)S(1)}, s32[2048]{0:T(1024)}, u32[]{:S(2)}) copy-start(s32[2048]{0:T(1024)} %param.13) | copy-start | bytes 24580
  15.6 9.7 %copy-start.2 = (f32[4,2048]{1,0:T(4,128)S(1)}, f32[4,2048]{1,0:T(4,128)}, u32[]{:S(2)}) copy-start(f32[4,2048]{1,0:T(4,128)} %drive_ref.1) | copy-start | bytes 98308
  15.6 9.7 %copy-start.3 = (s32[4096]{0:T(1024)S(1)}, s32[4096]{0:T(1024)}, u32[]{:S(2)}) copy-start(s32[4096]{0:T(1024)} %param.14) | copy-start | bytes 49156
  15.6 9.7 %copy-start.4 = (s32[4096]{0:T(1024)S(1)}, s32[4096]{0:T(1024)}, u32[]{:S(2)}) copy-start(s32[4096]{0:T(1024)} %param.15) | copy-start | bytes 49156
  15.6 9.7 %copy-start.6 = (f32[2048]{0:T(1024)S(1)}, f32[2048]{0:T(1024)}, u32[]{:S(2)}) copy-start(f32[2048]{0:T(1024)} %param.11) | copy-start | bytes 24580
  15.6 14.9 %all-to-all-start.2 = ((f32[8,16,128]{2,1,0:T(8,128)}), f32[8,16,128]{2,1,0:T(8,128)S(1)}, u32[]{:S(2)}, u32[]{:S(2)}) async-start(f32[8,16,128]{2,1,0:T(8,128)} %bitcast.6), calls=%async_computation.2 | async-start | bytes 131072 | tf_op jit(solution)/shard_map/all_to_all | solution.py:222
  25.4 1.1 copy-start.1
  30.5 19.1 %copy-start.5 = (s32[4096]{0:T(1024)S(1)}, s32[4096]{0:T(1024)}, u32[]{:S(2)}) copy-start(s32[4096]{0:T(1024)} %param.16) | copy-start | bytes 49156
  30.5 19.1 %copy-start.7 = (bf16[4096]{0:T(1024)(128)(2,1)S(1)}, bf16[4096]{0:T(1024)(128)(2,1)}, u32[]{:S(2)}) copy-start(bf16[4096]{0:T(1024)(128)(2,1)} %param.17) | copy-start | bytes 24580
  30.5 19.1 %copy-start.8 = (bf16[4096]{0:T(1024)(128)(2,1)S(1)}, bf16[4096]{0:T(1024)(128)(2,1)}, u32[]{:S(2)}) copy-start(bf16[4096]{0:T(1024)(128)(2,1)} %param.18) | copy-start | bytes 24580
  84.1 9.8 %all-to-all-start.4 = ((f32[8,40,128]{2,1,0:T(8,128)}), f32[8,40,128]{2,1,0:T(8,128)S(1)}, u32[]{:S(2)}, u32[]{:S(2)}) async-start(f32[8,40,128]{2,1,0:T(8,128)} %get-tuple-element.11), calls=%async_computation.4 | async-start | bytes 327680 | tf_op jit(solution)/shard_map/all_to_all | solution.py:222

commit v2 on v1

v2 whole, which is shorter than its diff:
```python
import jax
import jax.numpy as jnp
from jax import lax
from jax.experimental import pallas as pl
from jax.experimental.pallas import tpu as pltpu
from jax.sharding import PartitionSpec as P

REACH = 2
NS_ITERS = 3

F32 = jnp.float32
BF16 = jnp.bfloat16
EXACT = lax.Precision.HIGHEST
VMEM_LIMIT = 40 * 1024 * 1024
FORECAST_VMEM = 62 * 1024 * 1024

MEM = 16
OWN = 4
LAYERS = 40
LANE = 128
ROWS = OWN * LAYERS
MEMBERS = MEM * OWN
PARTS = 4
PART_COLS = 2048 // PARTS
SLOT_ROWS = 32
PACK = 40


def call(kernel, out_shape, scratch, flops, nbytes, *args, where=pltpu.VMEM, vmem=VMEM_LIMIT):
    block = pl.BlockSpec(memory_space=pltpu.VMEM)
    return pl.pallas_call(
        kernel,
        out_shape=out_shape,
        in_specs=[pl.BlockSpec(memory_space=where)] * len(args),
        out_specs=jax.tree.map(lambda _: block, out_shape),
        scratch_shapes=scratch,
        compiler_params=pltpu.CompilerParams(vmem_limit_bytes=vmem),
        cost_estimate=pl.CostEstimate(flops=flops, bytes_accessed=nbytes, transcendentals=0),
    )(*args)


def forecast_kernel(*refs):
    sources, (states_ref, seen_ref, table, seen, *buffers, done) = refs[:6], refs[6:]
    copies = [
        pltpu.make_async_copy(source, buffer, done.at[i])
        for i, (source, buffer) in enumerate(zip(sources, buffers))
    ]
    for copy in copies:
        copy.start()
    for copy in copies:
        copy.wait()
    x_ref, mix_ref, drive_ref, land_ref, pos_ref, field_ref = buffers
    layer = lax.broadcasted_iota(jnp.int32, (LAYERS, LANE), 0)
    for block in range(MEM):
        lanes = slice(block * LANE, (block + 1) * LANE)
        mix = mix_ref[block : block + 1, :]
        land = jnp.broadcast_to(land_ref[block : block + 1, :], (LAYERS, LANE)) > 0
        members = []
        for k in range(OWN):
            x = x_ref[k, :, lanes].astype(F32)
            above = jnp.where(layer == 0, x, pltpu.roll(x, 1, 0))
            below = jnp.where(layer == LAYERS - 1, x, pltpu.roll(x, LAYERS - 1, 0))
            stepped = x + mix * (above - 2.0 * x + below) - 0.05 * x * x * x
            stepped = jnp.where(layer == 0, stepped + drive_ref[k : k + 1, lanes], stepped)
            members.append(jnp.where(land, stepped, x))
        result = jnp.concatenate(members, axis=0).astype(BF16)
        states_ref[block] = result
        part, place = divmod(block, MEM // PARTS)
        table[part * ROWS : (part + 1) * ROWS, place * LANE : (place + 1) * LANE] = result

    column = lax.broadcasted_iota(jnp.int32, (PART_COLS, LANE), 0)
    for pair in range(SLOT_ROWS // 2):
        hot, codes = [], []
        for row in (2 * pair, 2 * pair + 1):
            pos = pos_ref[row : row + 1, :]
            hot.append(jnp.where(column == (pos & (PART_COLS - 1)), 1.0, 0.0).astype(BF16))
            codes.append((pos // PART_COLS) * LAYERS + field_ref[row : row + 1, :])
        found = jnp.dot(table[...], jnp.concatenate(hot, axis=1), preferred_element_type=F32)
        for i in range(2):
            hits = [layer == codes[i] - part * LAYERS for part in range(PARTS)]
            for k in range(OWN):
                total = jnp.zeros((LAYERS, LANE), F32)
                for part in range(PARTS):
                    first = part * ROWS + k * LAYERS
                    total = jnp.where(
                        hits[part],
                        found[first : first + LAYERS, i * LANE : (i + 1) * LANE],
                        total,
                    )
                at = k * SLOT_ROWS + 2 * pair + i
                seen[at : at + 1, :] = jnp.sum(total, axis=0, keepdims=True)
    values = seen[...].astype(BF16)
    for device in range(MEM):
        seen_ref[device] = values


def sums_kernel(
    seen_ref, own_ref, near_ref, far_ref, value_ref, error_ref, valid_ref,
    own_sum, near_sum, far_sum, wide, dev_s, inn_s, scaled,
):
    weights = (own_ref, near_ref.at[0], near_ref.at[1], far_ref.at[0], far_ref.at[1])
    wide[...] = seen_ref[...].reshape(MEMBERS * SLOT_ROWS, LANE).astype(F32)
    obs_value = value_ref[...].astype(F32)
    base = valid_ref[...].astype(F32) / error_ref[...].astype(F32)
    first_row = lax.broadcasted_iota(jnp.int32, (16, LANE), 0) == 0
    for row in range(SLOT_ROWS):
        lanes = slice(row * LANE, (row + 1) * LANE)
        values = wide[pl.ds(row, MEMBERS, stride=SLOT_ROWS), :]
        mean = jnp.sum(values, axis=0, keepdims=True) * (1.0 / MEMBERS)
        deviation = values - mean
        rounded = deviation.astype(BF16)
        dev_s[0:MEMBERS, lanes] = rounded
        dev_s[MEMBERS : 2 * MEMBERS, lanes] = rounded
        innovation = obs_value[row : row + 1, :] - mean
        inn_s[:, lanes] = jnp.where(first_row, innovation, 0.0).astype(BF16)
        for j in range(5):
            rinv = base[row : row + 1, :] * weights[j][row : row + 1, :]
            scaled[j * MEMBERS : (j + 1) * MEMBERS, lanes] = (deviation * rinv).astype(BF16)
    last = (((1,), (1,)), ((), ()))
    spread = lax.dot_general(scaled[...], dev_s[...], last, preferred_element_type=F32)
    pulled = lax.dot_general(inn_s[...], scaled[...], last, preferred_element_type=F32)
    left = lax.broadcasted_iota(jnp.int32, (32, LANE), 1) < MEMBERS
    outs = (own_sum, near_sum.at[0], near_sum.at[1], far_sum.at[0], far_sum.at[1])
    for j, out in enumerate(outs):
        top = spread[j * MEMBERS : j * MEMBERS + 32, :]
        bottom = spread[j * MEMBERS + 32 : (j + 1) * MEMBERS, :]
        out[0:32, :] = jnp.where(left, top, bottom)
        pull = pulled[0:8, j * MEMBERS : (j + 1) * MEMBERS]
        out[32:40, :] = jnp.concatenate([pull, pull], axis=1)


def regroup_kernel(states_ref, out_ref, wide):
    wide[...] = states_ref[...].reshape(MEM * ROWS, LANE).astype(F32)
    for layer in range(LAYERS):
        out_ref[:, layer * LANE : (layer + 1) * LANE] = wide[
            pl.ds(layer, MEMBERS, stride=LAYERS), :
        ].astype(BF16)


def exact_dot(a, b):
    return jnp.dot(a, b, precision=EXACT, preferred_element_type=F32)


def update_kernel(own_ref, near_ref, far_ref, rest_ref, states_ref, land_ref, out_ref, wide):
    block = lax.axis_index("mem")
    total = own_ref[...] + near_ref[0] + far_ref[0] + rest_ref[...]
    total = total * (1.0 / (MEMBERS - 1.0))
    upper = total[0:32, :]
    spread = jnp.concatenate([upper, pltpu.roll(upper, MEMBERS, 1)], axis=0)[:, :MEMBERS]
    pull = total[32:40, :MEMBERS]

    rows = lax.broadcasted_iota(jnp.int32, (MEMBERS, MEMBERS), 0)
    cols = lax.broadcasted_iota(jnp.int32, (MEMBERS, MEMBERS), 1)
    identity = jnp.where(rows == cols, 1.0, 0.0)
    system = identity + spread
    square = jnp.sum(jnp.sum(system * system, axis=1, keepdims=True), axis=0, keepdims=True)
    inv_scale = lax.rsqrt(square)
    current = system * inv_scale
    root = 1.5 * identity - 0.5 * current
    current = exact_dot(current, root)
    for sweep in range(1, NS_ITERS):
        middle = 1.5 * identity - 0.5 * exact_dot(root, current)
        if sweep < NS_ITERS - 1:
            current = exact_dot(current, middle)
        root = exact_dot(middle, root)
    inv_root = root * jnp.sqrt(inv_scale)
    mean_weight = exact_dot(exact_dot(pull, inv_root), inv_root)[0:1, :]
    turned = inv_root + mean_weight
    turned = turned + (1.0 - jnp.sum(turned, axis=1, keepdims=True)) * (1.0 / MEMBERS)
    high = turned.astype(BF16)
    low = (turned - high.astype(F32)).astype(BF16)
    both = jnp.concatenate([high, low], axis=0)
    land = jnp.broadcast_to(land_ref[pl.ds(block, 1), :], (MEMBERS, LANE)) > 0
    moved = jnp.dot(both, states_ref[...], preferred_element_type=F32)
    for layer in range(LAYERS):
        lanes = slice(layer * LANE, (layer + 1) * LANE)
        result = jnp.where(
            land,
            moved[:MEMBERS, lanes] + moved[MEMBERS:, lanes],
            states_ref[:, lanes].astype(F32),
        )
        wide[pl.ds(layer, MEMBERS, stride=LAYERS), :] = result
    out_ref[...] = wide[...].astype(BF16).reshape(MEM, ROWS, LANE)


def shape(*dims, dtype=BF16):
    return jax.ShapeDtypeStruct(dims, dtype)


def to_tile(value, steps):
    mem, tiles = lax.axis_size("mem"), lax.axis_size("tile")
    pairs = [
        (m * tiles + t, m * tiles + (t + (steps if m % 2 else -steps)) % tiles)
        for m in range(mem)
        for t in range(tiles)
    ]
    return lax.ppermute(value, ("mem", "tile"), pairs)


def to_other_core(value):
    return lax.ppermute(value, "mem", [(m, m ^ 1) for m in range(lax.axis_size("mem"))])


def on_device(
    ensemble_profiles_before,
    mixing_coefficient,
    surface_driver,
    terrain_indicator,
    measured_profile_position,
    measured_field_index,
    obs_valid,
    obs_value,
    obs_error,
    local_weight,
):
    land = terrain_indicator.reshape(MEM, LANE)
    slabs = local_weight.reshape(2 * REACH + 1, SLOT_ROWS, LANE)

    inputs = (
        ensemble_profiles_before,
        mixing_coefficient.reshape(MEM, LANE),
        surface_driver,
        land,
        measured_profile_position.reshape(SLOT_ROWS, LANE),
        measured_field_index.reshape(SLOT_ROWS, LANE),
    )
    states, seen = call(
        forecast_kernel,
        (shape(MEM, ROWS, LANE), shape(MEM, OWN * SLOT_ROWS, LANE)),
        [pltpu.VMEM((PARTS * ROWS, PART_COLS), BF16), pltpu.VMEM((OWN * SLOT_ROWS, LANE), F32)]
        + [pltpu.VMEM(array.shape, array.dtype) for array in inputs]
        + [pltpu.SemaphoreType.DMA((len(inputs),))],
        2 * 4096 * ROWS * 2048,
        2000000,
        *inputs,
        where=pl.ANY,
        vmem=FORECAST_VMEM,
    )
    slabs, seen = lax.optimization_barrier((slabs, seen))
    ahead = lax.axis_index("mem") % 2 == 1
    lower, upper = slabs[REACH - 1 :: -1][:REACH], slabs[REACH + 1 :]
    kept, given = jnp.where(ahead, lower, upper), jnp.where(ahead, upper, lower)
    taken = to_other_core(given)
    weights = [
        to_tile(jnp.stack([kept[d - 1], taken[d - 1]]), -d) for d in range(1, REACH + 1)
    ]
    seen = lax.all_to_all(seen, "mem", 0, 0, tiled=True)
    states, seen, weights = lax.optimization_barrier((states, seen, weights))
    states = lax.all_to_all(states, "mem", 0, 0, tiled=True)

    sums = call(
        sums_kernel,
        (shape(PACK, LANE, dtype=F32),) + (shape(2, PACK, LANE, dtype=F32),) * REACH,
        [
            pltpu.VMEM((MEMBERS * SLOT_ROWS, LANE), F32),
            pltpu.VMEM((2 * MEMBERS, SLOT_ROWS * LANE), BF16),
            pltpu.VMEM((16, SLOT_ROWS * LANE), BF16),
            pltpu.VMEM((5 * MEMBERS, SLOT_ROWS * LANE), BF16),
        ],
        2 * 768 * 128 * 2048,
        1000000,
        seen,
        slabs[REACH],
        *weights,
        obs_value.reshape(SLOT_ROWS, LANE),
        obs_error.reshape(SLOT_ROWS, LANE),
        obs_valid.reshape(SLOT_ROWS, LANE),
    )
    own = sums[0]
    near, far = [to_tile(part, d) for d, part in enumerate(sums[1:], 1)]
    rest = to_other_core(near[1] + far[1])
    states = call(
        regroup_kernel,
        shape(MEMBERS, LAYERS * LANE),
        [pltpu.VMEM((MEM * ROWS, LANE), F32)],
        MEM * ROWS * LANE,
        1300000,
        states,
    )
    analysed = call(
        update_kernel,
        shape(MEM, ROWS, LANE),
        [pltpu.VMEM((MEM * ROWS, LANE), F32)],
        2 * 128 * 64 * 5120,
        1300000,
        own,
        near,
        far,
        rest,
        states,
        land,
    )
    analysed = lax.all_to_all(analysed, "mem", 0, 0, tiled=True)
    return (
        analysed.reshape(MEM, OWN, LAYERS, LANE)
        .transpose(1, 2, 0, 3)
        .reshape(OWN, LAYERS, MEM * LANE)
    )


def solution(mesh):
    in_specs = (
        P("mem", None, "tile"),
        P("tile"),
        P("mem", "tile"),
        P("tile"),
        P("tile"),
        P("tile"),
        P("tile"),
        P("tile"),
        P("tile"),
        P("mem", "tile", None),
    )
    out_specs = P("mem", None, "tile")
    return jax.shard_map(
        on_device, mesh=mesh, in_specs=in_specs, out_specs=out_specs, check_vma=False
    )
```

time: 121 us -> 93.2 us (0.77)
  blocking collectives: 88.5 us -> 25.3 us
  starting transfers between devices: 16.4 us -> 41.1 us
  waiting for transfers between devices: 2.76 us -> 13.7 us
  local copies, waits for them, and re-layouts: 3.65 us -> 1.73 us
  Pallas kernels: 9.02 us -> 10.5 us
    all_to_all x4 -> x0, blocking collectives: 65 us -> none  [the longest x1 24.2 us: on_device(): states = lax.all_to_all(states, 'mem', 0, 0, tiled=True)]
    ppermute x0 -> x6, starting transfers between devices: none -> 23.7 us  [the longest x4 17.5 us: to_tile(): return lax.ppermute(value, ('mem', 'tile'), pairs)]
    ppermute x0 -> x6, waiting for transfers between devices: none -> 11.1 us  [the longest x4 10.2 us: to_tile(): return lax.ppermute(value, ('mem', 'tile'), pairs)]
    all_to_all x1, blocking collectives: 23.5 us -> 25.3 us  [on_device(): analysed = lax.all_to_all(analysed, 'mem', 0, 0, tiled=True)]
    dynamic_slice x1 -> x0, local copies, waits for them, and re-layouts: 1.51 us -> none  [on_device(): lax.dynamic_slice_in_dim(slabs, 3 - place2, GROUP)]
    pallas_call x4, Pallas kernels: 9.02 us -> 10.5 us  [call(): pl.pallas_call(kernel, out_shape=out_shape, in_specs=[pl.BlockSpec(memory...]
  transfers between devices with their start and end apart: 2 -> 8, of which waited for: 1 -> 5; matrix products, arithmetic and copies ran while one was open for 0% -> 0% of each run, Pallas kernels for 4% -> 3%
where the time goes in v2:
time: 93.2 us; the launch traced here: 92.6 us
  starting transfers between devices  41.1 us (44%)
  blocking collectives  25.3 us (27%)
  waiting for transfers between devices  13.7 us (15%)
  Pallas kernels  10.5 us (11%)
  local copies, waits for them, and re-layouts  1.73 us (2%)
    all_to_all x1, blocking collectives, on_device(): analysed = lax.all_to_all(analysed, 'mem', 0, 0, tiled=True)  25.3 us
    ppermute x4, starting transfers between devices, to_tile(): return lax.ppermute(value, ('mem', 'tile'), pairs)  17.5 us
    pallas_call x4, Pallas kernels, call(): pl.pallas_call(kernel, out_shape=out_shape, in_specs=[pl.BlockSpec(memory...  10.5 us
    all_to_all x1, starting transfers between devices, on_device(): seen = lax.all_to_all(seen, 'mem', 0, 0, tiled=True)  10.4 us
    ppermute x4, waiting for transfers between devices, to_tile(): return lax.ppermute(value, ('mem', 'tile'), pairs)  10.2 us
    all_to_all x1, starting transfers between devices, on_device(): states = lax.all_to_all(states, 'mem', 0, 0, tiled=True)  6.99 us
    ppermute x2, starting transfers between devices, to_other_core(): lax.ppermute(value, 'mem', [(m, m ^ 1) for m in range(lax.axis_size('mem'...  6.24 us
    all_to_all x1, waiting for transfers between devices, on_device(): states = lax.all_to_all(states, 'mem', 0, 0, tiled=True)  2.62 us
  transfers between devices with their start and end apart: 8, of which 5 were waited for; matrix products, arithmetic and copies ran while one was open for 0% of the time, Pallas kernels for 3%

profile of v2, /device:TPU:1, one launch (start us, length us, event | category | flops | bytes accessed | tf_op | source)
XLA Modules:
  0.0 92.6 jit_solution(13242677863282253459)
XLA Ops:
  0.0 6.0 %shard_map.100 = (bf16[16,160,128]{2,1,0:T(8,128)(2,1)}, bf16[16,128,128]{2,1,0:T(8,128)(2,1)}) custom-call(bf16[4,40,2048]{2,1,0:T(8,128)(2,1)} %refs_0_.1, f32[16,128]{1,0:T(8,128)} %bitcast.30, f32[4,2048]{1,0:T(4,128)} %refs_2_.1, s32[16,128]{1,0:T(8,128)} %bitcast.19, s32[32,128]{1,0:T(8,128)} %bitcast.28, s32[32,128]{1,0:T(8,128)} %bitcast.29), custom_call_target="tpu_custom_call" | custom-call | flops 2684354560 | bytes 2000000 | tf_op jit(solution)/shard_map/pallas_call | solution.py:31
  6.0 0.0 copy-start.4
  6.0 10.4 %all-to-all-start = ((bf16[16,128,128]{2,1,0:T(8,128)(2,1)}), bf16[16,128,128]{2,1,0:T(8,128)(2,1)S(1)}, u32[]{:S(2)}, u32[]{:S(2)}) async-start(bf16[16,128,128]{2,1,0:T(8,128)(2,1)} %get-tuple-element.18), calls=%async_computation | async-start | bytes 1048576 | tf_op jit(solution)/shard_map/all_to_all | solution.py:247
  16.4 0.0 copy-done.4
  16.4 2.1 %collective-permute-start = (f32[2,32,128]{2,1,0:T(8,128)S(1)}, f32[2,32,128]{2,1,0:T(8,128)S(1)}, u32[]{:S(2)}, u32[]{:S(2)}) collective-permute-start(f32[2,32,128]{2,1,0:T(8,128)S(1)} %get-tuple-element.28), channel_id=1, source_target_pairs={{0,32},{32,0},{64,96},{96,64},{128,160},{160,128},{192,224},{224,1... | collective-permute-start | bytes 98312 | tf_op jit(solution)/shard_map/ppermute | solution.py:201
  18.6 0.9 %collective-permute-done = f32[2,32,128]{2,1,0:T(8,128)S(1)} collective-permute-done((f32[2,32,128]{2,1,0:T(8,128)S(1)}, f32[2,32,128]{2,1,0:T(8,128)S(1)}, u32[]{:S(2)}, u32[]{:S(2)}) %collective-permute-start) | collective-permute-done | bytes 32800 | tf_op jit(solution)/shard_map/ppermute | solution.py:201
  19.5 11.2 %collective-permute-start.1 = (f32[2,32,128]{2,1,0:T(8,128)S(1)}, f32[2,32,128]{2,1,0:T(8,128)S(1)}, u32[]{:S(2)}, u32[]{:S(2)}) collective-permute-start(f32[2,32,128]{2,1,0:T(8,128)S(1)} %pad_maximum_fusion), channel_id=1, source_target_pairs={{0,1},{1,2},{2,3},{3,4},{4,5},{5,6},{6,7},{7,8},{8,9},{9,10},{10,1... | collective-permute-start | bytes 98312 | tf_op jit(solution)/shard_map/ppermute | solution.py:197
  30.8 2.4 %collective-permute-start.2 = (f32[2,32,128]{2,1,0:T(8,128)S(1)}, f32[2,32,128]{2,1,0:T(8,128)S(1)}, u32[]{:S(2)}, u32[]{:S(2)}) collective-permute-start(f32[2,32,128]{2,1,0:T(8,128)S(1)} %pad_maximum_fusion.1), channel_id=1, source_target_pairs={{0,2},{1,3},{2,4},{3,5},{4,6},{5,7},{6,8},{7,9},{8,10},{9,11},{10,... | collective-permute-start | bytes 98312 | tf_op jit(solution)/shard_map/ppermute | solution.py:197
  33.2 0.0 collective-permute-done.1.near_ref
  33.2 3.7 %collective-permute-done.2.far_ref = f32[2,32,128]{2,1,0:T(8,128)S(1)} collective-permute-done((f32[2,32,128]{2,1,0:T(8,128)S(1)}, f32[2,32,128]{2,1,0:T(8,128)S(1)}, u32[]{:S(2)}, u32[]{:S(2)}) %collective-permute-start.2) | collective-permute-done | bytes 32800 | tf_op jit(solution)/shard_map/ppermute | solution.py:197
  36.9 0.0 all-to-all-done.seen_ref
  37.0 7.0 %all-to-all-start.1 = ((bf16[16,160,128]{2,1,0:T(8,128)(2,1)}), bf16[16,160,128]{2,1,0:T(8,128)(2,1)S(1)}, u32[]{:S(2)}, u32[]{:S(2)}) async-start(bf16[16,160,128]{2,1,0:T(8,128)(2,1)} %get-tuple-element.26), calls=%async_computation.1 | async-start | bytes 1310720 | tf_op jit(solution)/shard_map/all_to_all | solution.py:249
  43.9 0.0 copy-start.1
  43.9 0.0 copy-start.2
  44.0 0.0 copy-start.3
  44.0 0.7 copy-done.1
  44.7 0.0 copy-done.2
  44.7 0.0 copy-done.3
  44.7 2.3 %shard_map.101 = (f32[40,128]{1,0:T(8,128)S(1)}, f32[2,40,128]{2,1,0:T(8,128)S(1)}, f32[2,40,128]{2,1,0:T(8,128)S(1)}) custom-call(bf16[16,128,128]{2,1,0:T(8,128)(2,1)S(1)} %all-to-all-done.seen_ref, f32[32,128]{1,0:T(8,128)S(1)} %slice_bitcast_fusion.own_ref, f32[2,32,128]{2,1,0:T(8,128)S(1)} %collective-permute-done.1.near_ref, ...), custom_call_target="tpu_custom_call" | custom-call | flops 402653184 | bytes 1000000 | tf_op jit(solution)/shard_map/pallas_call | solution.py:31
  46.9 1.9 %collective-permute-start.3 = (f32[2,40,128]{2,1,0:T(8,128)S(1)}, f32[2,40,128]{2,1,0:T(8,128)S(1)}, u32[]{:S(2)}, u32[]{:S(2)}) collective-permute-start(f32[2,40,128]{2,1,0:T(8,128)S(1)} %get-tuple-element.24), channel_id=1, source_target_pairs={{0,31},{1,0},{2,1},{3,2},{4,3},{5,4},{6,5},{7,6},{8,7},{9,8},{10,9... | collective-permute-start | bytes 122888 | tf_op jit(solution)/shard_map/ppermute | solution.py:197
  48.9 1.9 %collective-permute-start.4 = (f32[2,40,128]{2,1,0:T(8,128)S(1)}, f32[2,40,128]{2,1,0:T(8,128)S(1)}, u32[]{:S(2)}, u32[]{:S(2)}) collective-permute-start(f32[2,40,128]{2,1,0:T(8,128)S(1)} %get-tuple-element.25), channel_id=1, source_target_pairs={{0,30},{1,31},{2,0},{3,1},{4,2},{5,3},{6,4},{7,5},{8,6},{9,7},{10,... | collective-permute-start | bytes 122888 | tf_op jit(solution)/shard_map/ppermute | solution.py:197
  50.8 4.5 %collective-permute-done.3.near_ref = f32[2,40,128]{2,1,0:T(8,128)S(1)} collective-permute-done((f32[2,40,128]{2,1,0:T(8,128)S(1)}, f32[2,40,128]{2,1,0:T(8,128)S(1)}, u32[]{:S(2)}, u32[]{:S(2)}) %collective-permute-start.3) | collective-permute-done | bytes 40992 | tf_op jit(solution)/shard_map/ppermute | solution.py:197
  55.3 1.9 %collective-permute-done.4.far_ref = f32[2,40,128]{2,1,0:T(8,128)S(1)} collective-permute-done((f32[2,40,128]{2,1,0:T(8,128)S(1)}, f32[2,40,128]{2,1,0:T(8,128)S(1)}, u32[]{:S(2)}, u32[]{:S(2)}) %collective-permute-start.4) | collective-permute-done | bytes 40992 | tf_op jit(solution)/shard_map/ppermute | solution.py:197
  57.2 0.0 copy-start
  57.2 4.1 %collective-permute-start.5 = (f32[40,128]{1,0:T(8,128)S(1)}, f32[40,128]{1,0:T(8,128)S(1)}, u32[]{:S(2)}, u32[]{:S(2)}) collective-permute-start(f32[40,128]{1,0:T(8,128)S(1)} %fusion), channel_id=1, source_target_pairs={{0,32},{32,0},{64,96},{96,64},{128,160},{160,128},{192,224},{224,1... | collective-permute-start | bytes 61448 | tf_op jit(solution)/shard_map/ppermute | solution.py:201
  61.3 2.6 %all-to-all-done.1.states_ref = bf16[16,160,128]{2,1,0:T(8,128)(2,1)S(1)} async-done(((bf16[16,160,128]{2,1,0:T(8,128)(2,1)}), bf16[16,160,128]{2,1,0:T(8,128)(2,1)S(1)}, u32[]{:S(2)}, u32[]{:S(2)}) %all-to-all-start.1) | async-done | bytes 655392 | tf_op jit(solution)/shard_map/all_to_all | solution.py:249
  64.0 0.3 shard_map.102.states_ref
  64.3 0.0 collective-permute-done.5.rest_ref
  64.3 0.0 copy-done
  64.3 1.9 %shard_map.103 = bf16[16,160,128]{2,1,0:T(8,128)(2,1)S(1)} custom-call(f32[40,128]{1,0:T(8,128)S(1)} %get-tuple-element.23.own_ref, f32[2,40,128]{2,1,0:T(8,128)S(1)} %collective-permute-done.3.near_ref, f32[2,40,128]{2,1,0:T(8,128)S(1)} %collective-permute-done.4.far_ref, f32[40,128]{1,0:T(8,128)S(1)} %collective-permute-done.5.rest_ref, ...), custom_call_target="tpu_custom_call" | custom-call | flops 83886080 | bytes 1300000 | tf_op jit(solution)/shard_map/pallas_call | solution.py:31
  66.3 25.3 %all_to_all.15 = bf16[16,160,128]{2,1,0:T(8,128)(2,1)S(1)} all-to-all(bf16[16,160,128]{2,1,0:T(8,128)(2,1)S(1)} %shard_map.103), channel_id=1, replica_groups=mesh['mem'=16,'tile'=32] {'mem'}, dimensions={0} | all-to-all | bytes 1310720 | tf_op jit(solution)/shard_map/all_to_all | solution.py:293
  91.6 1.0 %copy.14 = bf16[16,4,5,8,128]{4,3,0,2,1:T(8,128)(2,1)} copy(bf16[16,4,5,8,128]{4,3,2,1,0:T(8,128)(2,1)S(1)} %bitcast.24) | data formatting | bytes 1310720 | tf_op jit(solution)/shard_map/reshape | solution.py:297
  (8 shorter events, 0.0 us)
Async XLA Ops:
  6.0 10.4 %copy-start.4 = (f32[1,1,20480]{2,1,0:T(1,128)S(1)}, f32[1,1,20480]{2,1,0:T(1,128)}, u32[]{:S(2)}) copy-start(f32[1,1,20480]{2,1,0:T(1,128)} %param.19) | copy-start | bytes 245764
  6.0 31.0 %all-to-all-start = ((bf16[16,128,128]{2,1,0:T(8,128)(2,1)}), bf16[16,128,128]{2,1,0:T(8,128)(2,1)S(1)}, u32[]{:S(2)}, u32[]{:S(2)}) async-start(bf16[16,128,128]{2,1,0:T(8,128)(2,1)} %get-tuple-element.18), calls=%async_computation | async-start | bytes 1048576 | tf_op jit(solution)/shard_map/all_to_all | solution.py:247
  16.4 3.1 %collective-permute-start = (f32[2,32,128]{2,1,0:T(8,128)S(1)}, f32[2,32,128]{2,1,0:T(8,128)S(1)}, u32[]{:S(2)}, u32[]{:S(2)}) collective-permute-start(f32[2,32,128]{2,1,0:T(8,128)S(1)} %get-tuple-element.28), channel_id=1, source_target_pairs={{0,32},{32,0},{64,96},{96,64},{128,160},{160,128},{192,224},{224,1... | collective-permute-start | bytes 98312 | tf_op jit(solution)/shard_map/ppermute | solution.py:201
  19.5 13.7 %collective-permute-start.1 = (f32[2,32,128]{2,1,0:T(8,128)S(1)}, f32[2,32,128]{2,1,0:T(8,128)S(1)}, u32[]{:S(2)}, u32[]{:S(2)}) collective-permute-start(f32[2,32,128]{2,1,0:T(8,128)S(1)} %pad_maximum_fusion), channel_id=1, source_target_pairs={{0,1},{1,2},{2,3},{3,4},{4,5},{5,6},{6,7},{7,8},{8,9},{9,10},{10,1... | collective-permute-start | bytes 98312 | tf_op jit(solution)/shard_map/ppermute | solution.py:197
  30.8 6.2 %collective-permute-start.2 = (f32[2,32,128]{2,1,0:T(8,128)S(1)}, f32[2,32,128]{2,1,0:T(8,128)S(1)}, u32[]{:S(2)}, u32[]{:S(2)}) collective-permute-start(f32[2,32,128]{2,1,0:T(8,128)S(1)} %pad_maximum_fusion.1), channel_id=1, source_target_pairs={{0,2},{1,3},{2,4},{3,5},{4,6},{5,7},{6,8},{7,9},{8,10},{9,11},{10,... | collective-permute-start | bytes 98312 | tf_op jit(solution)/shard_map/ppermute | solution.py:197
  37.0 27.0 %all-to-all-start.1 = ((bf16[16,160,128]{2,1,0:T(8,128)(2,1)}), bf16[16,160,128]{2,1,0:T(8,128)(2,1)S(1)}, u32[]{:S(2)}, u32[]{:S(2)}) async-start(bf16[16,160,128]{2,1,0:T(8,128)(2,1)} %get-tuple-element.26), calls=%async_computation.1 | async-start | bytes 1310720 | tf_op jit(solution)/shard_map/all_to_all | solution.py:249
  43.9 0.7 copy-start.1
  43.9 0.7 copy-start.2
  44.0 0.7 copy-start.3
  46.9 8.4 %collective-permute-start.3 = (f32[2,40,128]{2,1,0:T(8,128)S(1)}, f32[2,40,128]{2,1,0:T(8,128)S(1)}, u32[]{:S(2)}, u32[]{:S(2)}) collective-permute-start(f32[2,40,128]{2,1,0:T(8,128)S(1)} %get-tuple-element.24), channel_id=1, source_target_pairs={{0,31},{1,0},{2,1},{3,2},{4,3},{5,4},{6,5},{7,6},{8,7},{9,8},{10,9... | collective-permute-start | bytes 122888 | tf_op jit(solution)/shard_map/ppermute | solution.py:197
  48.9 8.4 %collective-permute-start.4 = (f32[2,40,128]{2,1,0:T(8,128)S(1)}, f32[2,40,128]{2,1,0:T(8,128)S(1)}, u32[]{:S(2)}, u32[]{:S(2)}) collective-permute-start(f32[2,40,128]{2,1,0:T(8,128)S(1)} %get-tuple-element.25), channel_id=1, source_target_pairs={{0,30},{1,31},{2,0},{3,1},{4,2},{5,3},{6,4},{7,5},{8,6},{9,7},{10,... | collective-permute-start | bytes 122888 | tf_op jit(solution)/shard_map/ppermute | solution.py:197
  57.2 7.1 %copy-start = (s32[2048]{0:T(1024)S(1)}, s32[2048]{0:T(1024)}, u32[]{:S(2)}) copy-start(s32[2048]{0:T(1024)} %param.13) | copy-start | bytes 24580
  57.2 7.1 %collective-permute-start.5 = (f32[40,128]{1,0:T(8,128)S(1)}, f32[40,128]{1,0:T(8,128)S(1)}, u32[]{:S(2)}, u32[]{:S(2)}) collective-permute-start(f32[40,128]{1,0:T(8,128)S(1)} %fusion), channel_id=1, source_target_pairs={{0,32},{32,0},{64,96},{96,64},{128,160},{160,128},{192,224},{224,1... | collective-permute-start | bytes 61448 | tf_op jit(solution)/shard_map/ppermute | solution.py:201

commit v3 on v2

--- a/solution.py
+++ b/solution.py
@@ -10,8 +10,8 @@
 
 F32 = jnp.float32
 BF16 = jnp.bfloat16
-EXACT = lax.Precision.HIGHEST
 VMEM_LIMIT = 40 * 1024 * 1024
+SUMS_FLOPS = 60_000_000_000
 FORECAST_VMEM = 62 * 1024 * 1024
 
 MEM = 16
@@ -27,11 +27,11 @@
 
 
 def call(kernel, out_shape, scratch, flops, nbytes, *args, where=pltpu.VMEM, vmem=VMEM_LIMIT):
-    block = pl.BlockSpec(memory_space=pltpu.VMEM)
+    block = pl.BlockSpec(memory_space=where)
     return pl.pallas_call(
         kernel,
         out_shape=out_shape,
-        in_specs=[pl.BlockSpec(memory_space=where)] * len(args),
+        in_specs=[block] * len(args),
         out_specs=jax.tree.map(lambda _: block, out_shape),
         scratch_shapes=scratch,
         compiler_params=pltpu.CompilerParams(vmem_limit_bytes=vmem),
@@ -40,7 +40,7 @@
 
 
 def forecast_kernel(*refs):
-    sources, (states_ref, seen_ref, table, seen, *buffers, done) = refs[:6], refs[6:]
+    sources, (states_ref, seen_ref, table, seen, states, rounded, *buffers, done, sent) = refs[:6], refs[6:]
     copies = [
         pltpu.make_async_copy(source, buffer, done.at[i])
         for i, (source, buffer) in enumerate(zip(sources, buffers))
@@ -64,16 +64,20 @@
             stepped = jnp.where(layer == 0, stepped + drive_ref[k : k + 1, lanes], stepped)
             members.append(jnp.where(land, stepped, x))
         result = jnp.concatenate(members, axis=0).astype(BF16)
-        states_ref[block] = result
+        states[block] = result
         part, place = divmod(block, MEM // PARTS)
         table[part * ROWS : (part + 1) * ROWS, place * LANE : (place + 1) * LANE] = result
 
-    column = lax.broadcasted_iota(jnp.int32, (PART_COLS, LANE), 0)
+    out_copies = [pltpu.make_async_copy(states, states_ref, sent.at[MEM])]
+    out_copies[0].start()
+
+    column = lax.broadcasted_iota(jnp.int32, (PART_COLS, LANE), 0).astype(jnp.int16)
     for pair in range(SLOT_ROWS // 2):
         hot, codes = [], []
         for row in (2 * pair, 2 * pair + 1):
             pos = pos_ref[row : row + 1, :]
-            hot.append(jnp.where(column == (pos & (PART_COLS - 1)), 1.0, 0.0).astype(BF16))
+            place = (pos & (PART_COLS - 1)).astype(jnp.int16)
+            hot.append(jnp.where(column == place, jnp.ones((), BF16), jnp.zeros((), BF16)))
             codes.append((pos // PART_COLS) * LAYERS + field_ref[row : row + 1, :])
         found = jnp.dot(table[...], jnp.concatenate(hot, axis=1), preferred_element_type=F32)
         for i in range(2):
@@ -89,44 +93,47 @@
                     )
                 at = k * SLOT_ROWS + 2 * pair + i
                 seen[at : at + 1, :] = jnp.sum(total, axis=0, keepdims=True)
-    values = seen[...].astype(BF16)
+    rounded[...] = seen[...].astype(BF16)
     for device in range(MEM):
-        seen_ref[device] = values
+        copy = pltpu.make_async_copy(rounded, seen_ref.at[device], sent.at[device])
+        copy.start()
+        out_copies.append(copy)
+    for copy in out_copies:
+        copy.wait()
 
 
 def sums_kernel(
-    seen_ref, own_ref, near_ref, far_ref, value_ref, error_ref, valid_ref,
-    own_sum, near_sum, far_sum, wide, dev_s, inn_s, scaled,
+    seen_ref, own_ref, near_ref, far_ref, value_ref, base_ref,
+    own_sum, near_sum, far_sum, wide, terms, scaled,
 ):
     weights = (own_ref, near_ref.at[0], near_ref.at[1], far_ref.at[0], far_ref.at[1])
     wide[...] = seen_ref[...].reshape(MEMBERS * SLOT_ROWS, LANE).astype(F32)
-    obs_value = value_ref[...].astype(F32)
-    base = valid_ref[...].astype(F32) / error_ref[...].astype(F32)
+    obs_value, base = value_ref[...], base_ref[...]
     first_row = lax.broadcasted_iota(jnp.int32, (16, LANE), 0) == 0
     for row in range(SLOT_ROWS):
         lanes = slice(row * LANE, (row + 1) * LANE)
         values = wide[pl.ds(row, MEMBERS, stride=SLOT_ROWS), :]
         mean = jnp.sum(values, axis=0, keepdims=True) * (1.0 / MEMBERS)
         deviation = values - mean
-        rounded = deviation.astype(BF16)
-        dev_s[0:MEMBERS, lanes] = rounded
-        dev_s[MEMBERS : 2 * MEMBERS, lanes] = rounded
+        terms[0:MEMBERS, lanes] = deviation.astype(BF16)
         innovation = obs_value[row : row + 1, :] - mean
-        inn_s[:, lanes] = jnp.where(first_row, innovation, 0.0).astype(BF16)
+        terms[MEMBERS:, lanes] = jnp.where(first_row, innovation, 0.0).astype(BF16)
         for j in range(5):
             rinv = base[row : row + 1, :] * weights[j][row : row + 1, :]
             scaled[j * MEMBERS : (j + 1) * MEMBERS, lanes] = (deviation * rinv).astype(BF16)
     last = (((1,), (1,)), ((), ()))
-    spread = lax.dot_general(scaled[...], dev_s[...], last, preferred_element_type=F32)
-    pulled = lax.dot_general(inn_s[...], scaled[...], last, preferred_element_type=F32)
+    sums = lax.dot_general(terms[...], scaled[...], last, preferred_element_type=F32)
     left = lax.broadcasted_iota(jnp.int32, (32, LANE), 1) < MEMBERS
     outs = (own_sum, near_sum.at[0], near_sum.at[1], far_sum.at[0], far_sum.at[1])
     for j, out in enumerate(outs):
-        top = spread[j * MEMBERS : j * MEMBERS + 32, :]
-        bottom = spread[j * MEMBERS + 32 : (j + 1) * MEMBERS, :]
-        out[0:32, :] = jnp.where(left, top, bottom)
-        pull = pulled[0:8, j * MEMBERS : (j + 1) * MEMBERS]
-        out[32:40, :] = jnp.concatenate([pull, pull], axis=1)
+        first = j // 2 * LANE
+        part = sums[:, first : min(first + LANE, 5 * MEMBERS)]
+        if j == 4:
+            part = jnp.concatenate([part, part], axis=1)
+        turned = pltpu.roll(part, MEMBERS, 1)
+        direct, moved = (part, turned) if j % 2 == 0 else (turned, part)
+        out[0:32, :] = jnp.where(left, direct[0:32, :], moved[32:64, :])
+        out[32:40, :] = direct[64:72, :]
 
 
 def regroup_kernel(states_ref, out_ref, wide):
@@ -137,8 +144,17 @@
         ].astype(BF16)
 
 
-def exact_dot(a, b):
-    return jnp.dot(a, b, precision=EXACT, preferred_element_type=F32)
+def split(value):
+    high = value.astype(BF16)
+    return high, (value - high.astype(F32)).astype(BF16)
+
+
+def split_dot(a, b):
+    a_high, a_low = split(a)
+    b_high, b_low = split(b)
+    left = jnp.concatenate([a_high, a_high, a_low], axis=1)
+    right = jnp.concatenate([b_high, b_low, b_high], axis=0)
+    return jnp.dot(left, right, preferred_element_type=F32)
 
 
 def update_kernel(own_ref, near_ref, far_ref, rest_ref, states_ref, land_ref, out_ref, wide):
@@ -157,19 +173,17 @@
     inv_scale = lax.rsqrt(square)
     current = system * inv_scale
     root = 1.5 * identity - 0.5 * current
-    current = exact_dot(current, root)
+    current = split_dot(current, root)
     for sweep in range(1, NS_ITERS):
-        middle = 1.5 * identity - 0.5 * exact_dot(root, current)
+        middle = 1.5 * identity - 0.5 * split_dot(root, current)
         if sweep < NS_ITERS - 1:
-            current = exact_dot(current, middle)
-        root = exact_dot(middle, root)
+            current = split_dot(current, middle)
+        root = split_dot(middle, root)
     inv_root = root * jnp.sqrt(inv_scale)
-    mean_weight = exact_dot(exact_dot(pull, inv_root), inv_root)[0:1, :]
+    mean_weight = split_dot(split_dot(pull, inv_root), inv_root)[0:1, :]
     turned = inv_root + mean_weight
     turned = turned + (1.0 - jnp.sum(turned, axis=1, keepdims=True)) * (1.0 / MEMBERS)
-    high = turned.astype(BF16)
-    low = (turned - high.astype(F32)).astype(BF16)
-    both = jnp.concatenate([high, low], axis=0)
+    both = jnp.concatenate(split(turned), axis=0)
     land = jnp.broadcast_to(land_ref[pl.ds(block, 1), :], (MEMBERS, LANE)) > 0
     moved = jnp.dot(both, states_ref[...], preferred_element_type=F32)
     for layer in range(LAYERS):
@@ -228,15 +242,21 @@
         forecast_kernel,
         (shape(MEM, ROWS, LANE), shape(MEM, OWN * SLOT_ROWS, LANE)),
         [pltpu.VMEM((PARTS * ROWS, PART_COLS), BF16), pltpu.VMEM((OWN * SLOT_ROWS, LANE), F32)]
+        + [pltpu.VMEM((MEM, ROWS, LANE), BF16), pltpu.VMEM((OWN * SLOT_ROWS, LANE), BF16)]
         + [pltpu.VMEM(array.shape, array.dtype) for array in inputs]
-        + [pltpu.SemaphoreType.DMA((len(inputs),))],
+        + [pltpu.SemaphoreType.DMA((len(inputs),)), pltpu.SemaphoreType.DMA((MEM + 1,))],
         2 * 4096 * ROWS * 2048,
         2000000,
         *inputs,
         where=pl.ANY,
         vmem=FORECAST_VMEM,
     )
-    slabs, seen = lax.optimization_barrier((slabs, seen))
+    slabs, obs_value, obs_error, obs_valid, seen = lax.optimization_barrier(
+        (slabs, obs_value, obs_error, obs_valid, seen)
+    )
+    own_weight = slabs[REACH]
+    value = obs_value.astype(F32).reshape(SLOT_ROWS, LANE)
+    base = (obs_valid.astype(F32) / obs_error.astype(F32)).reshape(SLOT_ROWS, LANE)
     ahead = lax.axis_index("mem") % 2 == 1
     lower, upper = slabs[REACH - 1 :: -1][:REACH], slabs[REACH + 1 :]
     kept, given = jnp.where(ahead, lower, upper), jnp.where(ahead, upper, lower)
@@ -245,7 +265,9 @@
         to_tile(jnp.stack([kept[d - 1], taken[d - 1]]), -d) for d in range(1, REACH + 1)
     ]
     seen = lax.all_to_all(seen, "mem", 0, 0, tiled=True)
-    states, seen, weights = lax.optimization_barrier((states, seen, weights))
+    states, seen, taken, own_weight, value, base = lax.optimization_barrier(
+        (states, seen, taken, own_weight, value, base)
+    )
     states = lax.all_to_all(states, "mem", 0, 0, tiled=True)
 
     sums = call(
@@ -253,18 +275,16 @@
         (shape(PACK, LANE, dtype=F32),) + (shape(2, PACK, LANE, dtype=F32),) * REACH,
         [
             pltpu.VMEM((MEMBERS * SLOT_ROWS, LANE), F32),
-            pltpu.VMEM((2 * MEMBERS, SLOT_ROWS * LANE), BF16),
-            pltpu.VMEM((16, SLOT_ROWS * LANE), BF16),
+            pltpu.VMEM((MEMBERS + 16, SLOT_ROWS * LANE), BF16),
             pltpu.VMEM((5 * MEMBERS, SLOT_ROWS * LANE), BF16),
         ],
-        2 * 768 * 128 * 2048,
+        SUMS_FLOPS,
         1000000,
         seen,
-        slabs[REACH],
+        own_weight,
         *weights,
-        obs_value.reshape(SLOT_ROWS, LANE),
-        obs_error.reshape(SLOT_ROWS, LANE),
-        obs_valid.reshape(SLOT_ROWS, LANE),
+        value,
+        base,
     )
     own = sums[0]
     near, far = [to_tile(part, d) for d, part in enumerate(sums[1:], 1)]

time: 93.2 us -> 91.7 us (0.984)
  waiting for transfers between devices: 13.7 us -> 7.52 us
  starting transfers between devices: 41.1 us -> 43.7 us
  blocking collectives: 25.3 us -> 27.5 us
    ppermute x4, waiting for transfers between devices: 10.2 us -> 6.37 us  [to_tile(): return lax.ppermute(value, ('mem', 'tile'), pairs)]
    ppermute x4, starting transfers between devices: 17.5 us -> 19.9 us  [to_tile(): return lax.ppermute(value, ('mem', 'tile'), pairs)]
    all_to_all x1, waiting for transfers between devices: 2.62 us -> 0.44 us  [on_device(): states = lax.all_to_all(states, 'mem', 0, 0, tiled=True)]
    all_to_all x1, blocking collectives: 25.3 us -> 27.5 us  [on_device(): analysed = lax.all_to_all(analysed, 'mem', 0, 0, tiled=True)]
where the time goes in v3:
time: 91.7 us; the launch traced here: 91 us
  starting transfers between devices  43.7 us (48%)
  blocking collectives  27.5 us (30%)
  Pallas kernels  10.3 us (11%)
  waiting for transfers between devices  7.52 us (8%)
  local copies, waits for them, and re-layouts  1.74 us (2%)
    all_to_all x1, blocking collectives, on_device(): analysed = lax.all_to_all(analysed, 'mem', 0, 0, tiled=True)  27.5 us
    ppermute x4, starting transfers between devices, to_tile(): return lax.ppermute(value, ('mem', 'tile'), pairs)  19.9 us
    all_to_all x1, starting transfers between devices, on_device(): seen = lax.all_to_all(seen, 'mem', 0, 0, tiled=True)  10.4 us
    pallas_call x4, Pallas kernels, call(): pl.pallas_call(kernel, out_shape=out_shape, in_specs=[block] * len(args),...  10.3 us
    ppermute x2, starting transfers between devices, to_other_core(): lax.ppermute(value, 'mem', [(m, m ^ 1) for m in range(lax.axis_size('mem'...  6.88 us
    all_to_all x1, starting transfers between devices, on_device(): states = lax.all_to_all(states, 'mem', 0, 0, tiled=True)  6.55 us
    ppermute x4, waiting for transfers between devices, to_tile(): return lax.ppermute(value, ('mem', 'tile'), pairs)  6.37 us
  transfers between devices with their start and end apart: 8, of which 5 were waited for; matrix products, arithmetic and copies ran while one was open for 0% of the time, Pallas kernels for 3%

profile of v3, /device:TPU:1, one launch (start us, length us, event | category | flops | bytes accessed | tf_op | source)
XLA Modules:
  0.0 91.0 jit_solution(4684163217315896723)
XLA Ops:
  0.0 5.9 %shard_map.100 = (bf16[16,160,128]{2,1,0:T(8,128)(2,1)}, bf16[16,128,128]{2,1,0:T(8,128)(2,1)}) custom-call(bf16[4,40,2048]{2,1,0:T(8,128)(2,1)} %refs_0_.1, f32[16,128]{1,0:T(8,128)} %bitcast.29, f32[4,2048]{1,0:T(4,128)} %refs_2_.1, s32[16,128]{1,0:T(8,128)} %bitcast.21, s32[32,128]{1,0:T(8,128)} %bitcast.27, s32[32,128]{1,0:T(8,128)} %bitcast.28), custom_call_target="tpu_custom_call" | custom-call | flops 2684354560 | bytes 2000000 | tf_op jit(solution)/shard_map/pallas_call | solution.py:31
  5.9 0.0 copy-start.1
  5.9 10.4 %all-to-all-start = ((bf16[16,128,128]{2,1,0:T(8,128)(2,1)}), bf16[16,128,128]{2,1,0:T(8,128)(2,1)S(1)}, u32[]{:S(2)}, u32[]{:S(2)}) async-start(bf16[16,128,128]{2,1,0:T(8,128)(2,1)} %get-tuple-element.22), calls=%async_computation | async-start | bytes 1048576 | tf_op jit(solution)/shard_map/all_to_all | solution.py:267
  16.3 0.0 copy-done.1
  16.3 2.1 %collective-permute-start = (f32[2,32,128]{2,1,0:T(8,128)S(1)}, f32[2,32,128]{2,1,0:T(8,128)S(1)}, u32[]{:S(2)}, u32[]{:S(2)}) collective-permute-start(f32[2,32,128]{2,1,0:T(8,128)S(1)} %get-tuple-element.36), channel_id=1, source_target_pairs={{0,32},{32,0},{64,96},{96,64},{128,160},{160,128},{192,224},{224,1... | collective-permute-start | bytes 98312 | tf_op jit(solution)/shard_map/ppermute | solution.py:215
  18.5 0.0 copy-start.2
  18.5 0.0 copy-start.3
  18.5 0.7 copy-done.2
  19.2 0.0 copy-done.3
  19.2 0.2 collective-permute-done
  19.4 11.2 %collective-permute-start.1 = (f32[2,32,128]{2,1,0:T(8,128)S(1)}, f32[2,32,128]{2,1,0:T(8,128)S(1)}, u32[]{:S(2)}, u32[]{:S(2)}) collective-permute-start(f32[2,32,128]{2,1,0:T(8,128)S(1)} %pad_maximum_fusion), channel_id=1, source_target_pairs={{0,1},{1,2},{2,3},{3,4},{4,5},{5,6},{6,7},{7,8},{8,9},{9,10},{10,1... | collective-permute-start | bytes 98312 | tf_op jit(solution)/shard_map/ppermute | solution.py:211
  30.7 0.0 copy-start.4
  30.7 2.4 %collective-permute-start.2 = (f32[2,32,128]{2,1,0:T(8,128)S(1)}, f32[2,32,128]{2,1,0:T(8,128)S(1)}, u32[]{:S(2)}, u32[]{:S(2)}) collective-permute-start(f32[2,32,128]{2,1,0:T(8,128)S(1)} %pad_maximum_fusion.1), channel_id=1, source_target_pairs={{0,2},{1,3},{2,4},{3,5},{4,6},{5,7},{6,8},{7,9},{8,10},{9,11},{10,... | collective-permute-start | bytes 98312 | tf_op jit(solution)/shard_map/ppermute | solution.py:211
  33.1 0.0 copy-done.4
  33.1 0.5 all-to-all-done.seen_ref
  33.6 6.5 %all-to-all-start.1 = ((bf16[16,160,128]{2,1,0:T(8,128)(2,1)}), bf16[16,160,128]{2,1,0:T(8,128)(2,1)S(1)}, u32[]{:S(2)}, u32[]{:S(2)}) async-start(bf16[16,160,128]{2,1,0:T(8,128)(2,1)} %get-tuple-element.34), calls=%async_computation.1 | async-start | bytes 1310720 | tf_op jit(solution)/shard_map/all_to_all | solution.py:271
  40.2 0.0 collective-permute-done.1.near_ref
  40.2 0.0 collective-permute-done.2.far_ref
  40.2 2.2 %shard_map.101 = (f32[40,128]{1,0:T(8,128)S(1)}, f32[2,40,128]{2,1,0:T(8,128)S(1)}, f32[2,40,128]{2,1,0:T(8,128)S(1)}) custom-call(bf16[16,128,128]{2,1,0:T(8,128)(2,1)S(1)} %all-to-all-done.seen_ref, f32[32,128]{1,0:T(8,128)S(1)} %slice_bitcast_fusion.own_ref, f32[2,32,128]{2,1,0:T(8,128)S(1)} %collective-permute-done.1.near_ref, ...), custom_call_target="tpu_custom_call" | custom-call | flops 60000002048 | bytes 1000000 | tf_op jit(solution)/shard_map/pallas_call | solution.py:31
  42.3 2.5 %collective-permute-start.3 = (f32[2,40,128]{2,1,0:T(8,128)S(1)}, f32[2,40,128]{2,1,0:T(8,128)S(1)}, u32[]{:S(2)}, u32[]{:S(2)}) collective-permute-start(f32[2,40,128]{2,1,0:T(8,128)S(1)} %get-tuple-element.32), channel_id=1, source_target_pairs={{0,31},{1,0},{2,1},{3,2},{4,3},{5,4},{6,5},{7,6},{8,7},{9,8},{10,9... | collective-permute-start | bytes 122888 | tf_op jit(solution)/shard_map/ppermute | solution.py:211
  44.9 3.8 %collective-permute-start.4 = (f32[2,40,128]{2,1,0:T(8,128)S(1)}, f32[2,40,128]{2,1,0:T(8,128)S(1)}, u32[]{:S(2)}, u32[]{:S(2)}) collective-permute-start(f32[2,40,128]{2,1,0:T(8,128)S(1)} %get-tuple-element.33), channel_id=1, source_target_pairs={{0,30},{1,31},{2,0},{3,1},{4,2},{5,3},{6,4},{7,5},{8,6},{9,7},{10,... | collective-permute-start | bytes 122888 | tf_op jit(solution)/shard_map/ppermute | solution.py:211
  48.6 3.6 %collective-permute-done.3.near_ref = f32[2,40,128]{2,1,0:T(8,128)S(1)} collective-permute-done((f32[2,40,128]{2,1,0:T(8,128)S(1)}, f32[2,40,128]{2,1,0:T(8,128)S(1)}, u32[]{:S(2)}, u32[]{:S(2)}) %collective-permute-start.3) | collective-permute-done | bytes 40992 | tf_op jit(solution)/shard_map/ppermute | solution.py:211
  52.2 2.8 %collective-permute-done.4.far_ref = f32[2,40,128]{2,1,0:T(8,128)S(1)} collective-permute-done((f32[2,40,128]{2,1,0:T(8,128)S(1)}, f32[2,40,128]{2,1,0:T(8,128)S(1)}, u32[]{:S(2)}, u32[]{:S(2)}) %collective-permute-start.4) | collective-permute-done | bytes 40992 | tf_op jit(solution)/shard_map/ppermute | solution.py:211
  55.0 0.0 copy-start
  55.0 4.7 %collective-permute-start.5 = (f32[40,128]{1,0:T(8,128)S(1)}, f32[40,128]{1,0:T(8,128)S(1)}, u32[]{:S(2)}, u32[]{:S(2)}) collective-permute-start(f32[40,128]{1,0:T(8,128)S(1)} %fusion), channel_id=1, source_target_pairs={{0,32},{32,0},{64,96},{96,64},{128,160},{160,128},{192,224},{224,1... | collective-permute-start | bytes 61448 | tf_op jit(solution)/shard_map/ppermute | solution.py:215
  59.7 0.4 all-to-all-done.1.states_ref
  60.2 0.3 shard_map.102.states_ref
  60.5 0.0 collective-permute-done.5.rest_ref
  60.6 0.0 copy-done
  60.6 2.0 %shard_map.103 = bf16[16,160,128]{2,1,0:T(8,128)(2,1)S(1)} custom-call(f32[40,128]{1,0:T(8,128)S(1)} %get-tuple-element.31.own_ref, f32[2,40,128]{2,1,0:T(8,128)S(1)} %collective-permute-done.3.near_ref, f32[2,40,128]{2,1,0:T(8,128)S(1)} %collective-permute-done.4.far_ref, f32[40,128]{1,0:T(8,128)S(1)} %collective-permute-done.5.rest_ref, ...), custom_call_target="tpu_custom_call" | custom-call | flops 83886080 | bytes 1300000 | tf_op jit(solution)/shard_map/pallas_call | solution.py:31
  62.5 27.5 %all_to_all.15 = bf16[16,160,128]{2,1,0:T(8,128)(2,1)S(1)} all-to-all(bf16[16,160,128]{2,1,0:T(8,128)(2,1)S(1)} %shard_map.103), channel_id=1, replica_groups=mesh['mem'=16,'tile'=32] {'mem'}, dimensions={0} | all-to-all | bytes 1310720 | tf_op jit(solution)/shard_map/all_to_all | solution.py:313
  90.0 1.0 %copy.14 = bf16[16,4,5,8,128]{4,3,0,2,1:T(8,128)(2,1)} copy(bf16[16,4,5,8,128]{4,3,2,1,0:T(8,128)(2,1)S(1)} %bitcast.23) | data formatting | bytes 1310720 | tf_op jit(solution)/shard_map/reshape | solution.py:317
  (10 shorter events, 0.1 us)
Async XLA Ops:
  5.9 10.4 %copy-start.1 = (f32[1,1,20480]{2,1,0:T(1,128)S(1)}, f32[1,1,20480]{2,1,0:T(1,128)}, u32[]{:S(2)}) copy-start(f32[1,1,20480]{2,1,0:T(1,128)} %param.19) | copy-start | bytes 245764
  5.9 27.7 %all-to-all-start = ((bf16[16,128,128]{2,1,0:T(8,128)(2,1)}), bf16[16,128,128]{2,1,0:T(8,128)(2,1)S(1)}, u32[]{:S(2)}, u32[]{:S(2)}) async-start(bf16[16,128,128]{2,1,0:T(8,128)(2,1)} %get-tuple-element.22), calls=%async_computation | async-start | bytes 1048576 | tf_op jit(solution)/shard_map/all_to_all | solution.py:267
  16.3 3.1 %collective-permute-start = (f32[2,32,128]{2,1,0:T(8,128)S(1)}, f32[2,32,128]{2,1,0:T(8,128)S(1)}, u32[]{:S(2)}, u32[]{:S(2)}) collective-permute-start(f32[2,32,128]{2,1,0:T(8,128)S(1)} %get-tuple-element.36), channel_id=1, source_target_pairs={{0,32},{32,0},{64,96},{96,64},{128,160},{160,128},{192,224},{224,1... | collective-permute-start | bytes 98312 | tf_op jit(solution)/shard_map/ppermute | solution.py:215
  18.5 0.7 copy-start.2
  18.5 0.7 copy-start.3
  19.4 20.7 %collective-permute-start.1 = (f32[2,32,128]{2,1,0:T(8,128)S(1)}, f32[2,32,128]{2,1,0:T(8,128)S(1)}, u32[]{:S(2)}, u32[]{:S(2)}) collective-permute-start(f32[2,32,128]{2,1,0:T(8,128)S(1)} %pad_maximum_fusion), channel_id=1, source_target_pairs={{0,1},{1,2},{2,3},{3,4},{4,5},{5,6},{6,7},{7,8},{8,9},{9,10},{10,1... | collective-permute-start | bytes 98312 | tf_op jit(solution)/shard_map/ppermute | solution.py:211
  30.7 2.5 %copy-start.4 = (bf16[4096]{0:T(1024)(128)(2,1)S(1)}, bf16[4096]{0:T(1024)(128)(2,1)}, u32[]{:S(2)}) copy-start(bf16[4096]{0:T(1024)(128)(2,1)} %param.17) | copy-start | bytes 24580
  30.7 9.5 %collective-permute-start.2 = (f32[2,32,128]{2,1,0:T(8,128)S(1)}, f32[2,32,128]{2,1,0:T(8,128)S(1)}, u32[]{:S(2)}, u32[]{:S(2)}) collective-permute-start(f32[2,32,128]{2,1,0:T(8,128)S(1)} %pad_maximum_fusion.1), channel_id=1, source_target_pairs={{0,2},{1,3},{2,4},{3,5},{4,6},{5,7},{6,8},{7,9},{8,10},{9,11},{10,... | collective-permute-start | bytes 98312 | tf_op jit(solution)/shard_map/ppermute | solution.py:211
  33.6 26.6 %all-to-all-start.1 = ((bf16[16,160,128]{2,1,0:T(8,128)(2,1)}), bf16[16,160,128]{2,1,0:T(8,128)(2,1)S(1)}, u32[]{:S(2)}, u32[]{:S(2)}) async-start(bf16[16,160,128]{2,1,0:T(8,128)(2,1)} %get-tuple-element.34), calls=%async_computation.1 | async-start | bytes 1310720 | tf_op jit(solution)/shard_map/all_to_all | solution.py:271
  42.3 9.8 %collective-permute-start.3 = (f32[2,40,128]{2,1,0:T(8,128)S(1)}, f32[2,40,128]{2,1,0:T(8,128)S(1)}, u32[]{:S(2)}, u32[]{:S(2)}) collective-permute-start(f32[2,40,128]{2,1,0:T(8,128)S(1)} %get-tuple-element.32), channel_id=1, source_target_pairs={{0,31},{1,0},{2,1},{3,2},{4,3},{5,4},{6,5},{7,6},{8,7},{9,8},{10,9... | collective-permute-start | bytes 122888 | tf_op jit(solution)/shard_map/ppermute | solution.py:211
  44.9 10.1 %collective-permute-start.4 = (f32[2,40,128]{2,1,0:T(8,128)S(1)}, f32[2,40,128]{2,1,0:T(8,128)S(1)}, u32[]{:S(2)}, u32[]{:S(2)}) collective-permute-start(f32[2,40,128]{2,1,0:T(8,128)S(1)} %get-tuple-element.33), channel_id=1, source_target_pairs={{0,30},{1,31},{2,0},{3,1},{4,2},{5,3},{6,4},{7,5},{8,6},{9,7},{10,... | collective-permute-start | bytes 122888 | tf_op jit(solution)/shard_map/ppermute | solution.py:211
  55.0 5.6 %copy-start = (s32[2048]{0:T(1024)S(1)}, s32[2048]{0:T(1024)}, u32[]{:S(2)}) copy-start(s32[2048]{0:T(1024)} %param.13) | copy-start | bytes 24580
  55.0 5.6 %collective-permute-start.5 = (f32[40,128]{1,0:T(8,128)S(1)}, f32[40,128]{1,0:T(8,128)S(1)}, u32[]{:S(2)}, u32[]{:S(2)}) collective-permute-start(f32[40,128]{1,0:T(8,128)S(1)} %fusion), channel_id=1, source_target_pairs={{0,32},{32,0},{64,96},{96,64},{128,160},{160,128},{192,224},{224,1... | collective-permute-start | bytes 61448 | tf_op jit(solution)/shard_map/ppermute | solution.py:215

commit v4 on v3

--- a/solution.py
+++ b/solution.py
@@ -157,7 +157,7 @@
     return jnp.dot(left, right, preferred_element_type=F32)
 
 
-def update_kernel(own_ref, near_ref, far_ref, rest_ref, states_ref, land_ref, out_ref, wide):
+def update_kernel(own_ref, far_ref, near_ref, rest_ref, states_ref, land_ref, out_ref, wide):
     block = lax.axis_index("mem")
     total = own_ref[...] + near_ref[0] + far_ref[0] + rest_ref[...]
     total = total * (1.0 / (MEMBERS - 1.0))
@@ -178,9 +178,11 @@
         middle = 1.5 * identity - 0.5 * split_dot(root, current)
         if sweep < NS_ITERS - 1:
             current = split_dot(current, middle)
+        else:
+            pull = split_dot(split_dot(pull, root), middle)
         root = split_dot(middle, root)
+    mean_weight = split_dot(pull, root)[0:1, :] * inv_scale
     inv_root = root * jnp.sqrt(inv_scale)
-    mean_weight = split_dot(split_dot(pull, inv_root), inv_root)[0:1, :]
     turned = inv_root + mean_weight
     turned = turned + (1.0 - jnp.sum(turned, axis=1, keepdims=True)) * (1.0 / MEMBERS)
     both = jnp.concatenate(split(turned), axis=0)
@@ -287,8 +289,9 @@
         base,
     )
     own = sums[0]
-    near, far = [to_tile(part, d) for d, part in enumerate(sums[1:], 1)]
-    rest = to_other_core(near[1] + far[1])
+    far = to_tile(sums[2], 2)
+    near = to_tile(sums[1], 1)
+    rest = to_other_core(far[1] + near[1])
     states = call(
         regroup_kernel,
         shape(MEMBERS, LAYERS * LANE),
@@ -304,8 +307,8 @@
         2 * 128 * 64 * 5120,
         1300000,
         own,
+        far,
         near,
-        far,
         rest,
         states,
         land,

time: 91.7 us -> 90.3 us (0.985)
  blocking collectives: 27.5 us -> 26.3 us
  starting transfers between devices: 43.7 us -> 42.7 us
  waiting for transfers between devices: 7.52 us -> 8.51 us
    all_to_all x1, waiting for transfers between devices: 0.44 us -> 1.69 us  [on_device(): states = lax.all_to_all(states, 'mem', 0, 0, tiled=True)]
    all_to_all x1, blocking collectives: 27.5 us -> 26.3 us  [on_device(): analysed = lax.all_to_all(analysed, 'mem', 0, 0, tiled=True)]
    ppermute x2, starting transfers between devices: 6.88 us -> 5.85 us  [to_other_core(): lax.ppermute(value, 'mem', [(m, m ^ 1) for m in range(lax.axis_size('mem'...]
where the time goes in v4:
time: 90.3 us; the launch traced here: 89.6 us
  starting transfers between devices  42.7 us (47%)
  blocking collectives  26.3 us (29%)
  Pallas kernels  10.2 us (11%)
  waiting for transfers between devices  8.51 us (9%)
  local copies, waits for them, and re-layouts  1.74 us (2%)
    all_to_all x1, blocking collectives, on_device(): analysed = lax.all_to_all(analysed, 'mem', 0, 0, tiled=True)  26.3 us
    ppermute x4, starting transfers between devices, to_tile(): return lax.ppermute(value, ('mem', 'tile'), pairs)  19.9 us
    all_to_all x1, starting transfers between devices, on_device(): seen = lax.all_to_all(seen, 'mem', 0, 0, tiled=True)  10.4 us
    pallas_call x4, Pallas kernels, call(): pl.pallas_call(kernel, out_shape=out_shape, in_specs=[block] * len(args),...  10.2 us
    all_to_all x1, starting transfers between devices, on_device(): states = lax.all_to_all(states, 'mem', 0, 0, tiled=True)  6.55 us
    ppermute x4, waiting for transfers between devices, to_tile(): return lax.ppermute(value, ('mem', 'tile'), pairs)  6.15 us
    ppermute x2, starting transfers between devices, to_other_core(): lax.ppermute(value, 'mem', [(m, m ^ 1) for m in range(lax.axis_size('mem'...  5.85 us
  transfers between devices with their start and end apart: 8, of which 5 were waited for; matrix products, arithmetic and copies ran while one was open for 0% of the time, Pallas kernels for 3%

profile of v4, /device:TPU:1, one launch (start us, length us, event | category | flops | bytes accessed | tf_op | source)
XLA Modules:
  0.0 89.6 jit_solution(7429927118517612995)
XLA Ops:
  0.0 5.9 %shard_map.100 = (bf16[16,160,128]{2,1,0:T(8,128)(2,1)}, bf16[16,128,128]{2,1,0:T(8,128)(2,1)}) custom-call(bf16[4,40,2048]{2,1,0:T(8,128)(2,1)} %refs_0_.1, f32[16,128]{1,0:T(8,128)} %bitcast.29, f32[4,2048]{1,0:T(4,128)} %refs_2_.1, s32[16,128]{1,0:T(8,128)} %bitcast.21, s32[32,128]{1,0:T(8,128)} %bitcast.27, s32[32,128]{1,0:T(8,128)} %bitcast.28), custom_call_target="tpu_custom_call" | custom-call | flops 2684354560 | bytes 2000000 | tf_op jit(solution)/shard_map/pallas_call | solution.py:31
  5.9 0.0 copy-start.1
  5.9 10.4 %all-to-all-start = ((bf16[16,128,128]{2,1,0:T(8,128)(2,1)}), bf16[16,128,128]{2,1,0:T(8,128)(2,1)S(1)}, u32[]{:S(2)}, u32[]{:S(2)}) async-start(bf16[16,128,128]{2,1,0:T(8,128)(2,1)} %get-tuple-element.22), calls=%async_computation | async-start | bytes 1048576 | tf_op jit(solution)/shard_map/all_to_all | solution.py:269
  16.3 0.0 copy-done.1
  16.3 2.1 %collective-permute-start = (f32[2,32,128]{2,1,0:T(8,128)S(1)}, f32[2,32,128]{2,1,0:T(8,128)S(1)}, u32[]{:S(2)}, u32[]{:S(2)}) collective-permute-start(f32[2,32,128]{2,1,0:T(8,128)S(1)} %get-tuple-element.36), channel_id=1, source_target_pairs={{0,32},{32,0},{64,96},{96,64},{128,160},{160,128},{192,224},{224,1... | collective-permute-start | bytes 98312 | tf_op jit(solution)/shard_map/ppermute | solution.py:217
  18.5 0.0 copy-start.2
  18.5 0.0 copy-start.3
  18.5 0.7 copy-done.2
  19.2 0.0 copy-done.3
  19.2 0.2 collective-permute-done
  19.4 11.2 %collective-permute-start.1 = (f32[2,32,128]{2,1,0:T(8,128)S(1)}, f32[2,32,128]{2,1,0:T(8,128)S(1)}, u32[]{:S(2)}, u32[]{:S(2)}) collective-permute-start(f32[2,32,128]{2,1,0:T(8,128)S(1)} %pad_maximum_fusion), channel_id=1, source_target_pairs={{0,1},{1,2},{2,3},{3,4},{4,5},{5,6},{6,7},{7,8},{8,9},{9,10},{10,1... | collective-permute-start | bytes 98312 | tf_op jit(solution)/shard_map/ppermute | solution.py:213
  30.7 0.0 copy-start.4
  30.7 2.4 %collective-permute-start.2 = (f32[2,32,128]{2,1,0:T(8,128)S(1)}, f32[2,32,128]{2,1,0:T(8,128)S(1)}, u32[]{:S(2)}, u32[]{:S(2)}) collective-permute-start(f32[2,32,128]{2,1,0:T(8,128)S(1)} %pad_maximum_fusion.1), channel_id=1, source_target_pairs={{0,2},{1,3},{2,4},{3,5},{4,6},{5,7},{6,8},{7,9},{8,10},{9,11},{10,... | collective-permute-start | bytes 98312 | tf_op jit(solution)/shard_map/ppermute | solution.py:213
  33.1 0.0 copy-done.4
  33.1 0.5 all-to-all-done.seen_ref
  33.6 6.5 %all-to-all-start.1 = ((bf16[16,160,128]{2,1,0:T(8,128)(2,1)}), bf16[16,160,128]{2,1,0:T(8,128)(2,1)S(1)}, u32[]{:S(2)}, u32[]{:S(2)}) async-start(bf16[16,160,128]{2,1,0:T(8,128)(2,1)} %get-tuple-element.34), calls=%async_computation.1 | async-start | bytes 1310720 | tf_op jit(solution)/shard_map/all_to_all | solution.py:273
  40.2 0.0 collective-permute-done.1.near_ref
  40.2 0.0 collective-permute-done.2.far_ref
  40.2 2.2 %shard_map.101 = (f32[40,128]{1,0:T(8,128)S(1)}, f32[2,40,128]{2,1,0:T(8,128)S(1)}, f32[2,40,128]{2,1,0:T(8,128)S(1)}) custom-call(bf16[16,128,128]{2,1,0:T(8,128)(2,1)S(1)} %all-to-all-done.seen_ref, f32[32,128]{1,0:T(8,128)S(1)} %slice_bitcast_fusion.own_ref, f32[2,32,128]{2,1,0:T(8,128)S(1)} %collective-permute-done.1.near_ref, ...), custom_call_target="tpu_custom_call" | custom-call | flops 60000002048 | bytes 1000000 | tf_op jit(solution)/shard_map/pallas_call | solution.py:31
  42.3 4.4 %collective-permute-start.3 = (f32[2,40,128]{2,1,0:T(8,128)S(1)}, f32[2,40,128]{2,1,0:T(8,128)S(1)}, u32[]{:S(2)}, u32[]{:S(2)}) collective-permute-start(f32[2,40,128]{2,1,0:T(8,128)S(1)} %get-tuple-element.32), channel_id=1, source_target_pairs={{0,30},{1,31},{2,0},{3,1},{4,2},{5,3},{6,4},{7,5},{8,6},{9,7},{10,... | collective-permute-start | bytes 122888 | tf_op jit(solution)/shard_map/ppermute | solution.py:213
  46.7 1.9 %collective-permute-start.4 = (f32[2,40,128]{2,1,0:T(8,128)S(1)}, f32[2,40,128]{2,1,0:T(8,128)S(1)}, u32[]{:S(2)}, u32[]{:S(2)}) collective-permute-start(f32[2,40,128]{2,1,0:T(8,128)S(1)} %get-tuple-element.33), channel_id=1, source_target_pairs={{0,31},{1,0},{2,1},{3,2},{4,3},{5,4},{6,5},{7,6},{8,7},{9,8},{10,9... | collective-permute-start | bytes 122888 | tf_op jit(solution)/shard_map/ppermute | solution.py:213
  48.6 3.7 %collective-permute-done.3.far_ref = f32[2,40,128]{2,1,0:T(8,128)S(1)} collective-permute-done((f32[2,40,128]{2,1,0:T(8,128)S(1)}, f32[2,40,128]{2,1,0:T(8,128)S(1)}, u32[]{:S(2)}, u32[]{:S(2)}) %collective-permute-start.3) | collective-permute-done | bytes 40992 | tf_op jit(solution)/shard_map/ppermute | solution.py:213
  52.3 2.5 %collective-permute-done.4.near_ref = f32[2,40,128]{2,1,0:T(8,128)S(1)} collective-permute-done((f32[2,40,128]{2,1,0:T(8,128)S(1)}, f32[2,40,128]{2,1,0:T(8,128)S(1)}, u32[]{:S(2)}, u32[]{:S(2)}) %collective-permute-start.4) | collective-permute-done | bytes 40992 | tf_op jit(solution)/shard_map/ppermute | solution.py:213
  54.8 0.0 copy-start
  54.8 3.7 %collective-permute-start.5 = (f32[40,128]{1,0:T(8,128)S(1)}, f32[40,128]{1,0:T(8,128)S(1)}, u32[]{:S(2)}, u32[]{:S(2)}) collective-permute-start(f32[40,128]{1,0:T(8,128)S(1)} %fusion), channel_id=1, source_target_pairs={{0,32},{32,0},{64,96},{96,64},{128,160},{160,128},{192,224},{224,1... | collective-permute-start | bytes 61448 | tf_op jit(solution)/shard_map/ppermute | solution.py:217
  58.5 1.7 %all-to-all-done.1.states_ref = bf16[16,160,128]{2,1,0:T(8,128)(2,1)S(1)} async-done(((bf16[16,160,128]{2,1,0:T(8,128)(2,1)}), bf16[16,160,128]{2,1,0:T(8,128)(2,1)S(1)}, u32[]{:S(2)}, u32[]{:S(2)}) %all-to-all-start.1) | async-done | bytes 655392 | tf_op jit(solution)/shard_map/all_to_all | solution.py:273
  60.2 0.3 shard_map.102.states_ref
  60.5 0.0 collective-permute-done.5.rest_ref
  60.5 0.0 copy-done
  60.5 1.8 %shard_map.103 = bf16[16,160,128]{2,1,0:T(8,128)(2,1)S(1)} custom-call(f32[40,128]{1,0:T(8,128)S(1)} %get-tuple-element.31.own_ref, f32[2,40,128]{2,1,0:T(8,128)S(1)} %collective-permute-done.3.far_ref, f32[2,40,128]{2,1,0:T(8,128)S(1)} %collective-permute-done.4.near_ref, f32[40,128]{1,0:T(8,128)S(1)} %collective-permute-done.5.rest_ref, ...), custom_call_target="tpu_custom_call" | custom-call | flops 83886080 | bytes 1300000 | tf_op jit(solution)/shard_map/pallas_call | solution.py:31
  62.3 26.3 %all_to_all.15 = bf16[16,160,128]{2,1,0:T(8,128)(2,1)S(1)} all-to-all(bf16[16,160,128]{2,1,0:T(8,128)(2,1)S(1)} %shard_map.103), channel_id=1, replica_groups=mesh['mem'=16,'tile'=32] {'mem'}, dimensions={0} | all-to-all | bytes 1310720 | tf_op jit(solution)/shard_map/all_to_all | solution.py:316
  88.6 1.0 %copy.14 = bf16[16,4,5,8,128]{4,3,0,2,1:T(8,128)(2,1)} copy(bf16[16,4,5,8,128]{4,3,2,1,0:T(8,128)(2,1)S(1)} %bitcast.23) | data formatting | bytes 1310720 | tf_op jit(solution)/shard_map/reshape | solution.py:320
  (10 shorter events, 0.1 us)
Async XLA Ops:
  5.9 10.4 %copy-start.1 = (f32[1,1,20480]{2,1,0:T(1,128)S(1)}, f32[1,1,20480]{2,1,0:T(1,128)}, u32[]{:S(2)}) copy-start(f32[1,1,20480]{2,1,0:T(1,128)} %param.19) | copy-start | bytes 245764
  5.9 27.7 %all-to-all-start = ((bf16[16,128,128]{2,1,0:T(8,128)(2,1)}), bf16[16,128,128]{2,1,0:T(8,128)(2,1)S(1)}, u32[]{:S(2)}, u32[]{:S(2)}) async-start(bf16[16,128,128]{2,1,0:T(8,128)(2,1)} %get-tuple-element.22), calls=%async_computation | async-start | bytes 1048576 | tf_op jit(solution)/shard_map/all_to_all | solution.py:269
  16.3 3.1 %collective-permute-start = (f32[2,32,128]{2,1,0:T(8,128)S(1)}, f32[2,32,128]{2,1,0:T(8,128)S(1)}, u32[]{:S(2)}, u32[]{:S(2)}) collective-permute-start(f32[2,32,128]{2,1,0:T(8,128)S(1)} %get-tuple-element.36), channel_id=1, source_target_pairs={{0,32},{32,0},{64,96},{96,64},{128,160},{160,128},{192,224},{224,1... | collective-permute-start | bytes 98312 | tf_op jit(solution)/shard_map/ppermute | solution.py:217
  18.5 0.7 copy-start.2
  18.5 0.7 copy-start.3
  19.4 20.7 %collective-permute-start.1 = (f32[2,32,128]{2,1,0:T(8,128)S(1)}, f32[2,32,128]{2,1,0:T(8,128)S(1)}, u32[]{:S(2)}, u32[]{:S(2)}) collective-permute-start(f32[2,32,128]{2,1,0:T(8,128)S(1)} %pad_maximum_fusion), channel_id=1, source_target_pairs={{0,1},{1,2},{2,3},{3,4},{4,5},{5,6},{6,7},{7,8},{8,9},{9,10},{10,1... | collective-permute-start | bytes 98312 | tf_op jit(solution)/shard_map/ppermute | solution.py:213
  30.7 2.5 %copy-start.4 = (bf16[4096]{0:T(1024)(128)(2,1)S(1)}, bf16[4096]{0:T(1024)(128)(2,1)}, u32[]{:S(2)}) copy-start(bf16[4096]{0:T(1024)(128)(2,1)} %param.17) | copy-start | bytes 24580
  30.7 9.5 %collective-permute-start.2 = (f32[2,32,128]{2,1,0:T(8,128)S(1)}, f32[2,32,128]{2,1,0:T(8,128)S(1)}, u32[]{:S(2)}, u32[]{:S(2)}) collective-permute-start(f32[2,32,128]{2,1,0:T(8,128)S(1)} %pad_maximum_fusion.1), channel_id=1, source_target_pairs={{0,2},{1,3},{2,4},{3,5},{4,6},{5,7},{6,8},{7,9},{8,10},{9,11},{10,... | collective-permute-start | bytes 98312 | tf_op jit(solution)/shard_map/ppermute | solution.py:213
  33.6 26.6 %all-to-all-start.1 = ((bf16[16,160,128]{2,1,0:T(8,128)(2,1)}), bf16[16,160,128]{2,1,0:T(8,128)(2,1)S(1)}, u32[]{:S(2)}, u32[]{:S(2)}) async-start(bf16[16,160,128]{2,1,0:T(8,128)(2,1)} %get-tuple-element.34), calls=%async_computation.1 | async-start | bytes 1310720 | tf_op jit(solution)/shard_map/all_to_all | solution.py:273
  42.3 10.0 %collective-permute-start.3 = (f32[2,40,128]{2,1,0:T(8,128)S(1)}, f32[2,40,128]{2,1,0:T(8,128)S(1)}, u32[]{:S(2)}, u32[]{:S(2)}) collective-permute-start(f32[2,40,128]{2,1,0:T(8,128)S(1)} %get-tuple-element.32), channel_id=1, source_target_pairs={{0,30},{1,31},{2,0},{3,1},{4,2},{5,3},{6,4},{7,5},{8,6},{9,7},{10,... | collective-permute-start | bytes 122888 | tf_op jit(solution)/shard_map/ppermute | solution.py:213
  46.7 8.1 %collective-permute-start.4 = (f32[2,40,128]{2,1,0:T(8,128)S(1)}, f32[2,40,128]{2,1,0:T(8,128)S(1)}, u32[]{:S(2)}, u32[]{:S(2)}) collective-permute-start(f32[2,40,128]{2,1,0:T(8,128)S(1)} %get-tuple-element.33), channel_id=1, source_target_pairs={{0,31},{1,0},{2,1},{3,2},{4,3},{5,4},{6,5},{7,6},{8,7},{9,8},{10,9... | collective-permute-start | bytes 122888 | tf_op jit(solution)/shard_map/ppermute | solution.py:213
  54.8 5.8 %copy-start = (s32[2048]{0:T(1024)S(1)}, s32[2048]{0:T(1024)}, u32[]{:S(2)}) copy-start(s32[2048]{0:T(1024)} %param.13) | copy-start | bytes 24580
  54.8 5.7 %collective-permute-start.5 = (f32[40,128]{1,0:T(8,128)S(1)}, f32[40,128]{1,0:T(8,128)S(1)}, u32[]{:S(2)}, u32[]{:S(2)}) collective-permute-start(f32[40,128]{1,0:T(8,128)S(1)} %fusion), channel_id=1, source_target_pairs={{0,32},{32,0},{64,96},{96,64},{128,160},{160,128},{192,224},{224,1... | collective-permute-start | bytes 61448 | tf_op jit(solution)/shard_map/ppermute | solution.py:217

commit v5 on v4

--- a/solution.py
+++ b/solution.py
@@ -136,14 +136,6 @@
         out[32:40, :] = direct[64:72, :]
 
 
-def regroup_kernel(states_ref, out_ref, wide):
-    wide[...] = states_ref[...].reshape(MEM * ROWS, LANE).astype(F32)
-    for layer in range(LAYERS):
-        out_ref[:, layer * LANE : (layer + 1) * LANE] = wide[
-            pl.ds(layer, MEMBERS, stride=LAYERS), :
-        ].astype(BF16)
-
-
 def split(value):
     high = value.astype(BF16)
     return high, (value - high.astype(F32)).astype(BF16)
@@ -157,7 +149,12 @@
     return jnp.dot(left, right, preferred_element_type=F32)
 
 
-def update_kernel(own_ref, far_ref, near_ref, rest_ref, states_ref, land_ref, out_ref, wide):
+def update_kernel(own_ref, far_ref, near_ref, rest_ref, received_ref, land_ref, out_ref, wide, states_ref):
+    wide[...] = received_ref[...].reshape(MEM * ROWS, LANE).astype(F32)
+    for layer in range(LAYERS):
+        states_ref[:, layer * LANE : (layer + 1) * LANE] = wide[
+            pl.ds(layer, MEMBERS, stride=LAYERS), :
+        ].astype(BF16)
     block = lax.axis_index("mem")
     total = own_ref[...] + near_ref[0] + far_ref[0] + rest_ref[...]
     total = total * (1.0 / (MEMBERS - 1.0))
@@ -292,18 +289,10 @@
     far = to_tile(sums[2], 2)
     near = to_tile(sums[1], 1)
     rest = to_other_core(far[1] + near[1])
-    states = call(
-        regroup_kernel,
-        shape(MEMBERS, LAYERS * LANE),
-        [pltpu.VMEM((MEM * ROWS, LANE), F32)],
-        MEM * ROWS * LANE,
-        1300000,
-        states,
-    )
     analysed = call(
         update_kernel,
         shape(MEM, ROWS, LANE),
-        [pltpu.VMEM((MEM * ROWS, LANE), F32)],
+        [pltpu.VMEM((MEM * ROWS, LANE), F32), pltpu.VMEM((MEMBERS, LAYERS * LANE), BF16)],
         2 * 128 * 64 * 5120,
         1300000,
         own,

time: 90.3 us -> 90.2 us (level)
    pallas_call x4 -> x3, Pallas kernels: 10.2 us -> 9.86 us  [call(): pl.pallas_call(kernel, out_shape=out_shape, in_specs=[block] * len(args),...]
  transfers between devices with their start and end apart: 8 -> 8, of which waited for: 5 -> 6; matrix products, arithmetic and copies ran while one was open for 0% -> 0% of each run, Pallas kernels for 3% -> 2%
where the time goes in v5:
time: 90.2 us; the launch traced here: 89.6 us
  starting transfers between devices  42.6 us (47%)
  blocking collectives  26.5 us (29%)
  Pallas kernels  9.86 us (11%)
  waiting for transfers between devices  8.62 us (10%)
  local copies, waits for them, and re-layouts  1.74 us (2%)
    all_to_all x1, blocking collectives, on_device(): analysed = lax.all_to_all(analysed, 'mem', 0, 0, tiled=True)  26.5 us
    ppermute x4, starting transfers between devices, to_tile(): return lax.ppermute(value, ('mem', 'tile'), pairs)  19.9 us
    all_to_all x1, starting transfers between devices, on_device(): seen = lax.all_to_all(seen, 'mem', 0, 0, tiled=True)  10.4 us
    pallas_call x3, Pallas kernels, call(): pl.pallas_call(kernel, out_shape=out_shape, in_specs=[block] * len(args),...  9.86 us
    all_to_all x1, starting transfers between devices, on_device(): states = lax.all_to_all(states, 'mem', 0, 0, tiled=True)  6.55 us
    ppermute x4, waiting for transfers between devices, to_tile(): return lax.ppermute(value, ('mem', 'tile'), pairs)  6.14 us
    ppermute x2, starting transfers between devices, to_other_core(): lax.ppermute(value, 'mem', [(m, m ^ 1) for m in range(lax.axis_size('mem'...  5.73 us
  transfers between devices with their start and end apart: 8, of which 6 were waited for; matrix products, arithmetic and copies ran while one was open for 0% of the time, Pallas kernels for 2%

profile of v5, /device:TPU:1, one launch (start us, length us, event | category | flops | bytes accessed | tf_op | source)
XLA Modules:
  0.0 89.6 jit_solution(15123995603713460863)
XLA Ops:
  0.0 5.9 %shard_map.100 = (bf16[16,160,128]{2,1,0:T(8,128)(2,1)}, bf16[16,128,128]{2,1,0:T(8,128)(2,1)}) custom-call(bf16[4,40,2048]{2,1,0:T(8,128)(2,1)} %refs_0_.1, f32[16,128]{1,0:T(8,128)} %bitcast.29, f32[4,2048]{1,0:T(4,128)} %refs_2_.1, s32[16,128]{1,0:T(8,128)} %bitcast.21, s32[32,128]{1,0:T(8,128)} %bitcast.27, s32[32,128]{1,0:T(8,128)} %bitcast.28), custom_call_target="tpu_custom_call" | custom-call | flops 2684354560 | bytes 2000000 | tf_op jit(solution)/shard_map/pallas_call | solution.py:31
  5.9 0.0 copy-start.1
  5.9 10.4 %all-to-all-start = ((bf16[16,128,128]{2,1,0:T(8,128)(2,1)}), bf16[16,128,128]{2,1,0:T(8,128)(2,1)S(1)}, u32[]{:S(2)}, u32[]{:S(2)}) async-start(bf16[16,128,128]{2,1,0:T(8,128)(2,1)} %get-tuple-element.22), calls=%async_computation | async-start | bytes 1048576 | tf_op jit(solution)/shard_map/all_to_all | solution.py:266
  16.3 0.0 copy-done.1
  16.3 2.1 %collective-permute-start = (f32[2,32,128]{2,1,0:T(8,128)S(1)}, f32[2,32,128]{2,1,0:T(8,128)S(1)}, u32[]{:S(2)}, u32[]{:S(2)}) collective-permute-start(f32[2,32,128]{2,1,0:T(8,128)S(1)} %get-tuple-element.36), channel_id=1, source_target_pairs={{0,32},{32,0},{64,96},{96,64},{128,160},{160,128},{192,224},{224,1... | collective-permute-start | bytes 98312 | tf_op jit(solution)/shard_map/ppermute | solution.py:214
  18.5 0.0 copy-start.2
  18.5 0.0 copy-start.3
  18.5 0.7 copy-done.2
  19.2 0.0 copy-done.3
  19.2 0.2 collective-permute-done
  19.4 11.2 %collective-permute-start.1 = (f32[2,32,128]{2,1,0:T(8,128)S(1)}, f32[2,32,128]{2,1,0:T(8,128)S(1)}, u32[]{:S(2)}, u32[]{:S(2)}) collective-permute-start(f32[2,32,128]{2,1,0:T(8,128)S(1)} %pad_maximum_fusion), channel_id=1, source_target_pairs={{0,1},{1,2},{2,3},{3,4},{4,5},{5,6},{6,7},{7,8},{8,9},{9,10},{10,1... | collective-permute-start | bytes 98312 | tf_op jit(solution)/shard_map/ppermute | solution.py:210
  30.7 0.0 copy-start.4
  30.7 2.4 %collective-permute-start.2 = (f32[2,32,128]{2,1,0:T(8,128)S(1)}, f32[2,32,128]{2,1,0:T(8,128)S(1)}, u32[]{:S(2)}, u32[]{:S(2)}) collective-permute-start(f32[2,32,128]{2,1,0:T(8,128)S(1)} %pad_maximum_fusion.1), channel_id=1, source_target_pairs={{0,2},{1,3},{2,4},{3,5},{4,6},{5,7},{6,8},{7,9},{8,10},{9,11},{10,... | collective-permute-start | bytes 98312 | tf_op jit(solution)/shard_map/ppermute | solution.py:210
  33.1 0.0 copy-done.4
  33.1 0.5 all-to-all-done.seen_ref
  33.6 6.5 %all-to-all-start.1 = ((bf16[16,160,128]{2,1,0:T(8,128)(2,1)}), bf16[16,160,128]{2,1,0:T(8,128)(2,1)S(1)}, u32[]{:S(2)}, u32[]{:S(2)}) async-start(bf16[16,160,128]{2,1,0:T(8,128)(2,1)} %get-tuple-element.34), calls=%async_computation.1 | async-start | bytes 1310720 | tf_op jit(solution)/shard_map/all_to_all | solution.py:270
  40.2 0.0 collective-permute-done.1.near_ref
  40.2 0.0 collective-permute-done.2.far_ref
  40.2 2.2 %shard_map.101 = (f32[40,128]{1,0:T(8,128)S(1)}, f32[2,40,128]{2,1,0:T(8,128)S(1)}, f32[2,40,128]{2,1,0:T(8,128)S(1)}) custom-call(bf16[16,128,128]{2,1,0:T(8,128)(2,1)S(1)} %all-to-all-done.seen_ref, f32[32,128]{1,0:T(8,128)S(1)} %slice_bitcast_fusion.own_ref, f32[2,32,128]{2,1,0:T(8,128)S(1)} %collective-permute-done.1.near_ref, ...), custom_call_target="tpu_custom_call" | custom-call | flops 60000002048 | bytes 1000000 | tf_op jit(solution)/shard_map/pallas_call | solution.py:31
  42.3 4.4 %collective-permute-start.3 = (f32[2,40,128]{2,1,0:T(8,128)S(1)}, f32[2,40,128]{2,1,0:T(8,128)S(1)}, u32[]{:S(2)}, u32[]{:S(2)}) collective-permute-start(f32[2,40,128]{2,1,0:T(8,128)S(1)} %get-tuple-element.32), channel_id=1, source_target_pairs={{0,30},{1,31},{2,0},{3,1},{4,2},{5,3},{6,4},{7,5},{8,6},{9,7},{10,... | collective-permute-start | bytes 122888 | tf_op jit(solution)/shard_map/ppermute | solution.py:210
  46.7 0.0 copy-start
  46.7 1.9 %collective-permute-start.4 = (f32[2,40,128]{2,1,0:T(8,128)S(1)}, f32[2,40,128]{2,1,0:T(8,128)S(1)}, u32[]{:S(2)}, u32[]{:S(2)}) collective-permute-start(f32[2,40,128]{2,1,0:T(8,128)S(1)} %get-tuple-element.33), channel_id=1, source_target_pairs={{0,31},{1,0},{2,1},{3,2},{4,3},{5,4},{6,5},{7,6},{8,7},{9,8},{10,9... | collective-permute-start | bytes 122888 | tf_op jit(solution)/shard_map/ppermute | solution.py:210
  48.6 3.7 %collective-permute-done.3.far_ref = f32[2,40,128]{2,1,0:T(8,128)S(1)} collective-permute-done((f32[2,40,128]{2,1,0:T(8,128)S(1)}, f32[2,40,128]{2,1,0:T(8,128)S(1)}, u32[]{:S(2)}, u32[]{:S(2)}) %collective-permute-start.3) | collective-permute-done | bytes 40992 | tf_op jit(solution)/shard_map/ppermute | solution.py:210
  52.3 2.5 %collective-permute-done.4.near_ref = f32[2,40,128]{2,1,0:T(8,128)S(1)} collective-permute-done((f32[2,40,128]{2,1,0:T(8,128)S(1)}, f32[2,40,128]{2,1,0:T(8,128)S(1)}, u32[]{:S(2)}, u32[]{:S(2)}) %collective-permute-start.4) | collective-permute-done | bytes 40992 | tf_op jit(solution)/shard_map/ppermute | solution.py:210
  54.8 3.6 %collective-permute-start.5 = (f32[40,128]{1,0:T(8,128)S(1)}, f32[40,128]{1,0:T(8,128)S(1)}, u32[]{:S(2)}, u32[]{:S(2)}) collective-permute-start(f32[40,128]{1,0:T(8,128)S(1)} %fusion), channel_id=1, source_target_pairs={{0,32},{32,0},{64,96},{96,64},{128,160},{160,128},{192,224},{224,1... | collective-permute-start | bytes 61448 | tf_op jit(solution)/shard_map/ppermute | solution.py:214
  58.4 0.8 collective-permute-done.5.rest_ref
  59.2 1.0 %all-to-all-done.1.received_ref = bf16[16,160,128]{2,1,0:T(8,128)(2,1)S(1)} async-done(((bf16[16,160,128]{2,1,0:T(8,128)(2,1)}), bf16[16,160,128]{2,1,0:T(8,128)(2,1)S(1)}, u32[]{:S(2)}, u32[]{:S(2)}) %all-to-all-start.1) | async-done | bytes 655392 | tf_op jit(solution)/shard_map/all_to_all | solution.py:270
  60.2 0.0 copy-done
  60.2 1.8 %shard_map.102 = bf16[16,160,128]{2,1,0:T(8,128)(2,1)S(1)} custom-call(f32[40,128]{1,0:T(8,128)S(1)} %get-tuple-element.31.own_ref, f32[2,40,128]{2,1,0:T(8,128)S(1)} %collective-permute-done.3.far_ref, f32[2,40,128]{2,1,0:T(8,128)S(1)} %collective-permute-done.4.near_ref, f32[40,128]{1,0:T(8,128)S(1)} %collective-permute-done.5.rest_ref, ...), custom_call_target="tpu_custom_call" | custom-call | flops 83886080 | bytes 1300000 | tf_op jit(solution)/shard_map/pallas_call | solution.py:31
  62.0 26.5 %all_to_all.15 = bf16[16,160,128]{2,1,0:T(8,128)(2,1)S(1)} all-to-all(bf16[16,160,128]{2,1,0:T(8,128)(2,1)S(1)} %shard_map.102), channel_id=1, replica_groups=mesh['mem'=16,'tile'=32] {'mem'}, dimensions={0} | all-to-all | bytes 1310720 | tf_op jit(solution)/shard_map/all_to_all | solution.py:305
  88.5 1.0 %copy.14 = bf16[16,4,5,8,128]{4,3,0,2,1:T(8,128)(2,1)} copy(bf16[16,4,5,8,128]{4,3,2,1,0:T(8,128)(2,1)S(1)} %bitcast.23) | data formatting | bytes 1310720 | tf_op jit(solution)/shard_map/reshape | solution.py:309
  (10 shorter events, 0.1 us)
Async XLA Ops:
  5.9 10.4 %copy-start.1 = (f32[1,1,20480]{2,1,0:T(1,128)S(1)}, f32[1,1,20480]{2,1,0:T(1,128)}, u32[]{:S(2)}) copy-start(f32[1,1,20480]{2,1,0:T(1,128)} %param.19) | copy-start | bytes 245764
  5.9 27.7 %all-to-all-start = ((bf16[16,128,128]{2,1,0:T(8,128)(2,1)}), bf16[16,128,128]{2,1,0:T(8,128)(2,1)S(1)}, u32[]{:S(2)}, u32[]{:S(2)}) async-start(bf16[16,128,128]{2,1,0:T(8,128)(2,1)} %get-tuple-element.22), calls=%async_computation | async-start | bytes 1048576 | tf_op jit(solution)/shard_map/all_to_all | solution.py:266
  16.3 3.1 %collective-permute-start = (f32[2,32,128]{2,1,0:T(8,128)S(1)}, f32[2,32,128]{2,1,0:T(8,128)S(1)}, u32[]{:S(2)}, u32[]{:S(2)}) collective-permute-start(f32[2,32,128]{2,1,0:T(8,128)S(1)} %get-tuple-element.36), channel_id=1, source_target_pairs={{0,32},{32,0},{64,96},{96,64},{128,160},{160,128},{192,224},{224,1... | collective-permute-start | bytes 98312 | tf_op jit(solution)/shard_map/ppermute | solution.py:214
  18.5 0.7 copy-start.2
  18.5 0.7 copy-start.3
  19.4 20.7 %collective-permute-start.1 = (f32[2,32,128]{2,1,0:T(8,128)S(1)}, f32[2,32,128]{2,1,0:T(8,128)S(1)}, u32[]{:S(2)}, u32[]{:S(2)}) collective-permute-start(f32[2,32,128]{2,1,0:T(8,128)S(1)} %pad_maximum_fusion), channel_id=1, source_target_pairs={{0,1},{1,2},{2,3},{3,4},{4,5},{5,6},{6,7},{7,8},{8,9},{9,10},{10,1... | collective-permute-start | bytes 98312 | tf_op jit(solution)/shard_map/ppermute | solution.py:210
  30.7 2.5 %copy-start.4 = (bf16[4096]{0:T(1024)(128)(2,1)S(1)}, bf16[4096]{0:T(1024)(128)(2,1)}, u32[]{:S(2)}) copy-start(bf16[4096]{0:T(1024)(128)(2,1)} %param.17) | copy-start | bytes 24580
  30.7 9.5 %collective-permute-start.2 = (f32[2,32,128]{2,1,0:T(8,128)S(1)}, f32[2,32,128]{2,1,0:T(8,128)S(1)}, u32[]{:S(2)}, u32[]{:S(2)}) collective-permute-start(f32[2,32,128]{2,1,0:T(8,128)S(1)} %pad_maximum_fusion.1), channel_id=1, source_target_pairs={{0,2},{1,3},{2,4},{3,5},{4,6},{5,7},{6,8},{7,9},{8,10},{9,11},{10,... | collective-permute-start | bytes 98312 | tf_op jit(solution)/shard_map/ppermute | solution.py:210
  33.6 26.6 %all-to-all-start.1 = ((bf16[16,160,128]{2,1,0:T(8,128)(2,1)}), bf16[16,160,128]{2,1,0:T(8,128)(2,1)S(1)}, u32[]{:S(2)}, u32[]{:S(2)}) async-start(bf16[16,160,128]{2,1,0:T(8,128)(2,1)} %get-tuple-element.34), calls=%async_computation.1 | async-start | bytes 1310720 | tf_op jit(solution)/shard_map/all_to_all | solution.py:270
  42.3 10.0 %collective-permute-start.3 = (f32[2,40,128]{2,1,0:T(8,128)S(1)}, f32[2,40,128]{2,1,0:T(8,128)S(1)}, u32[]{:S(2)}, u32[]{:S(2)}) collective-permute-start(f32[2,40,128]{2,1,0:T(8,128)S(1)} %get-tuple-element.32), channel_id=1, source_target_pairs={{0,30},{1,31},{2,0},{3,1},{4,2},{5,3},{6,4},{7,5},{8,6},{9,7},{10,... | collective-permute-start | bytes 122888 | tf_op jit(solution)/shard_map/ppermute | solution.py:210
  46.7 13.5 %copy-start = (s32[2048]{0:T(1024)S(1)}, s32[2048]{0:T(1024)}, u32[]{:S(2)}) copy-start(s32[2048]{0:T(1024)} %param.13) | copy-start | bytes 24580
  46.7 8.1 %collective-permute-start.4 = (f32[2,40,128]{2,1,0:T(8,128)S(1)}, f32[2,40,128]{2,1,0:T(8,128)S(1)}, u32[]{:S(2)}, u32[]{:S(2)}) collective-permute-start(f32[2,40,128]{2,1,0:T(8,128)S(1)} %get-tuple-element.33), channel_id=1, source_target_pairs={{0,31},{1,0},{2,1},{3,2},{4,3},{5,4},{6,5},{7,6},{8,7},{9,8},{10,9... | collective-permute-start | bytes 122888 | tf_op jit(solution)/shard_map/ppermute | solution.py:210
  54.8 4.4 %collective-permute-start.5 = (f32[40,128]{1,0:T(8,128)S(1)}, f32[40,128]{1,0:T(8,128)S(1)}, u32[]{:S(2)}, u32[]{:S(2)}) collective-permute-start(f32[40,128]{1,0:T(8,128)S(1)} %fusion), channel_id=1, source_target_pairs={{0,32},{32,0},{64,96},{96,64},{128,160},{160,128},{192,224},{224,1... | collective-permute-start | bytes 61448 | tf_op jit(solution)/shard_map/ppermute | solution.py:214
